TPU v7x, 256 devices: a whole 4x4x8 slice. The times are simulated.
256 devices in a mesh: tok: 4 (over z_lo), hid: 64 (over y, z_hi, x, core).
Axes of the slice: x: 4, y: 4, z: 8 (z_hi: 2, z_lo: 4; z = z_hi * 4 + z_lo), core: 2. Of those that a mesh axis runs over, the one named last changes fastest.
Arguments:
- tokens: bfloat16 [512, 8192], P('hid', 'tok'), may hold values from -20 to 20
- gate_weight: bfloat16 [8192, 26624], P('tok', 'hid'), may hold values from -0.0625 to 0.0625
- up_weight: bfloat16 [8192, 26624], P('tok', 'hid'), may hold values from -0.0625 to 0.0625
- down_weight: bfloat16 [26624, 8192], P('hid', 'tok'), may hold values from -0.0390625 to 0.0390625
- out_grad: bfloat16 [512, 8192], P('hid', 'tok'), may hold values from -6 to 6
- amax_prior: float32 [4], replicated, may hold values from 4 to 60
Outputs:
- output: bfloat16 [512, 8192], P('hid', 'tok')
- input_grad: bfloat16 [512, 8192], P('hid', 'tok')
- gate_grad: bfloat16 [8192, 26624], P('tok', 'hid')
- up_grad: bfloat16 [8192, 26624], P('tok', 'hid')
- down_grad: bfloat16 [26624, 8192], P('hid', 'tok')
- amaxes: float32 [6], replicated
All inputs are finite; a program needn't handle non-finite values. Where the computation divides by a largest or mean magnitude, that divisor is 1e-20 or more.
Results may differ from a plain program's by a relative error of at most 0.0081.
Values may be sent and summed in bfloat16 or wider, within the bound.
A program may use at most 128 MiB of HBM per device.

v0:
```python
import jax
import jax.numpy as jnp
from jax import lax
from jax.sharding import PartitionSpec as P


def quantize(value, scale):
    return jnp.clip(value / scale, -448.0, 448.0).astype(jnp.bfloat16)


def contract_last(left, right):
    return lax.dot_general(
        left, right, (((1,), (1,)), ((), ())), preferred_element_type=jnp.float32
    )


def contract_first(left, right):
    return lax.dot_general(
        left, right, (((0,), (0,)), ((), ())), preferred_element_type=jnp.float32
    )


def merged_max(value):
    return lax.pmax(value, ("tok", "hid"))


def shards(tokens, gate_weight, up_weight, down_weight, out_grad, amax_prior):
    scales = amax_prior / 448.0
    width = gate_weight.shape[1]
    local_x = jnp.max(jnp.abs(tokens.astype(jnp.float32)))
    xq = quantize(tokens.astype(jnp.float32), scales[0])
    xq_all = lax.all_gather(xq, "hid", axis=0, tiled=True)
    rows = xq_all
    both = (
        lax.psum_scatter(
            jnp.concatenate(
                [
                    jnp.dot(rows, gate_weight, preferred_element_type=jnp.float32),
                    jnp.dot(rows, up_weight, preferred_element_type=jnp.float32),
                ],
                axis=1,
            ),
            "tok",
            scatter_dimension=0,
            tiled=True,
        )
        * scales[0]
    )
    gate = both[:, :width]
    up = both[:, width:]
    sig = jax.nn.sigmoid(gate)
    act = gate * sig
    hidden = act * up
    local_h = jnp.max(jnp.abs(hidden))
    hq = quantize(hidden, scales[1])
    hq_all = lax.all_gather(hq, "tok", axis=0, tiled=True)
    rows = hq_all
    output = (
        lax.psum_scatter(
            jnp.dot(rows, down_weight, preferred_element_type=jnp.float32),
            "hid",
            scatter_dimension=0,
            tiled=True,
        )
        * scales[1]
    ).astype(jnp.bfloat16)
    local_g = jnp.max(jnp.abs(out_grad.astype(jnp.float32)))
    grad_q = quantize(out_grad.astype(jnp.float32), scales[2])
    grad_all = lax.all_gather(grad_q, "hid", axis=0, tiled=True)
    rows = grad_all
    dhidden = (
        lax.psum_scatter(contract_last(rows, down_weight), "tok", scatter_dimension=0, tiled=True)
        * scales[2]
    )
    dgate = dhidden * up * sig * (1.0 + gate * (1.0 - sig))
    dup = dhidden * act
    local_p = jnp.maximum(jnp.max(jnp.abs(dgate)), jnp.max(jnp.abs(dup)))
    dgq = quantize(dgate, scales[3])
    duq = quantize(dup, scales[3])
    dg_all, du_all = (
        lax.all_gather(dgq, "tok", axis=0, tiled=True),
        lax.all_gather(duq, "tok", axis=0, tiled=True),
    )
    input_sum = lax.psum_scatter(
        contract_last(dg_all, gate_weight), "hid", scatter_dimension=0, tiled=True
    ) + lax.psum_scatter(contract_last(du_all, up_weight), "hid", scatter_dimension=0, tiled=True)
    input_grad = (input_sum * scales[3]).astype(jnp.bfloat16)
    wgate = contract_first(xq_all, dg_all) * (scales[0] * scales[3])
    wup = contract_first(xq_all, du_all) * (scales[0] * scales[3])
    wdown = contract_first(hq_all, grad_all) * (scales[1] * scales[2])
    local_gu = jnp.maximum(jnp.max(jnp.abs(wgate)), jnp.max(jnp.abs(wup)))
    local_down = jnp.max(jnp.abs(wdown))
    merged_x = merged_max(local_x)
    merged_h = merged_max(local_h)
    merged_g = merged_max(local_g)
    merged_p = merged_max(local_p)
    grads_max = lax.pmax(jnp.stack([local_gu, local_down]), ("tok", "hid"))
    peaks = jnp.concatenate([jnp.stack([merged_x, merged_h, merged_g, merged_p]), grads_max])
    gate_grad = (wgate / (peaks[4] + 1e-06)).astype(jnp.bfloat16)
    up_grad = (wup / (peaks[4] + 1e-06)).astype(jnp.bfloat16)
    down_grad = (wdown / (peaks[5] + 1e-06)).astype(jnp.bfloat16)
    amaxes = jnp.log(peaks + 1e-06)
    return (output, input_grad, gate_grad, up_grad, down_grad, amaxes)


def solution(mesh):
    placed = (
        P("hid", "tok"),
        P("tok", "hid"),
        P("tok", "hid"),
        P("hid", "tok"),
        P("hid", "tok"),
        P(),
    )
    return jax.shard_map(
        shards,
        mesh=mesh,
        in_specs=placed,
        out_specs=(
            P("hid", "tok"),
            P("hid", "tok"),
            P("tok", "hid"),
            P("tok", "hid"),
            P("hid", "tok"),
            P(),
        ),
        check_vma=False,
    )
```

profile of v0, /device:TPU:1, one launch (start us, length us, event | category | flops | bytes accessed | tf_op | source)
XLA Modules:
  0.0 1119.5 jit_solution(16258862497696976997)
XLA Ops:
  7.2 0.8 broadcast_multiply_fusion.1
  8.0 0.7 fusion.8
  8.7 2.7 fusion.3
  11.4 2.6 fusion.6
  14.1 85.2 %all-gather.3.cloned.1.call-done = bf16[512,2048]{1,0:T(8,128)(2,1)} async-done(((bf16[8,2048]{1,0:T(8,128)(2,1)}), bf16[512,2048]{1,0:T(8,128)(2,1)}) %all-gather.3.cloned.1.call-update) | async-done | bytes 2097168 | tf_op jit(solution)/shard_map/all_gather | solution.py:32
  99.3 3.3 fusion.10
  102.7 1.1 fusion.9
  103.8 1.3 pad_maximum_fusion
  105.2 75.3 %all-gather.5.cloned.1.call-done = bf16[512,2048]{1,0:T(8,128)(2,1)} async-done(((bf16[8,2048]{1,0:T(8,128)(2,1)}), bf16[512,2048]{1,0:T(8,128)(2,1)}) %all-gather.5.cloned.1.call-update) | async-done | bytes 2097168 | tf_op jit(solution)/shard_map/all_gather | solution.py:69
  180.4 3.6 fusion.12
  184.1 35.6 %reduce-scatter.5.cloned.1.call-done = f32[128,832]{0,1:T(8,128)} async-done(((f32[512,832]{0,1:T(8,128)}), f32[128,832]{0,1:T(8,128)}) %reduce-scatter.5.cloned.1.call-update) | async-done | bytes 426000 | tf_op jit(solution)/shard_map/reduce_scatter | solution.py:35
  219.7 1.7 broadcast_multiply_fusion
  221.3 30.0 %reduce-scatter.9.cloned.1.call-done = f32[128,416]{0,1:T(8,128)} async-done(((f32[512,416]{0,1:T(8,128)}), f32[128,416]{0,1:T(8,128)}) %reduce-scatter.9.cloned.1.call-update) | async-done | bytes 213008 | tf_op jit(solution)/shard_map/reduce_scatter | solution.py:72
  251.4 3.6 abs_reduce_fusion.3
  255.6 11.1 all_gather.18
  266.8 12.7 %all_gather.19 = bf16[512,416]{0,1:T(8,128)(2,1)S(1)} all-gather(bf16[128,416]{0,1:T(8,128)(2,1)S(1)} %get-tuple-element.15), channel_id=1, replica_groups=mesh['tok'=4,'hid'=64] {'tok'}, dimensions={0}, use_global_device_ids=true | all-gather | bytes 532480 | tf_op jit(solution)/shard_map/all_gather | solution.py:82
  279.5 1.3 fusion.13
  281.0 3.3 convolution_add_fusion
  284.4 12.1 %all_gather.16 = bf16[512,416]{0,1:T(8,128)(2,1)S(1)} all-gather(bf16[128,416]{0,1:T(8,128)(2,1)S(1)} %get-tuple-element.18), channel_id=1, replica_groups=mesh['tok'=4,'hid'=64] {'tok'}, dimensions={0}, use_global_device_ids=true | all-gather | bytes 532480 | tf_op jit(solution)/shard_map/all_gather | solution.py:56
  296.5 4.7 fusion.11
  303.7 5.2 abs_reduce_fusion.2
  308.9 3.5 abs_reduce_fusion.1
  315.0 5.0 abs_reduce_fusion
  320.0 0.7 pad_maximum_fusion.1
  320.7 82.1 %all-reduce = (f32[2]{0:T(128)S(1)}, f32[1]{0:T(128)}, f32[1]{0:T(128)}, f32[1]{0:T(128)}, f32[1]{0:T(128)}) all-reduce(f32[2]{0:T(128)S(1)} %pad_maximum_fusion.1, f32[1]{0:T(128)} %bitcast.8, f32[1]{0:T(128)} %bitcast.9, f32[1]{0:T(128)} %bitcast.10, f32[1]{0:T(128)} %bitcast.11), channel_id=1, replica_groups=mesh['tok'=4,'hid'=64] {'tok','hid'}, use_global_device_ids=true, to_apply=%region_8.9 | all-reduce | flops 6 | bytes 48 | tf_op jit(solution)/shard_map/pmax | solution.py:97
  404.7 2.7 concatenate.7
  407.9 3.7 divide_convert_fusion
  411.7 4.6 divide_convert_fusion.1
  416.3 281.1 %reduce-scatter.11.cloned.1.call-done = f32[8,2048]{1,0:T(8,128)} async-done(((f32[512,2048]{1,0:T(8,128)}), f32[8,2048]{1,0:T(8,128)}) %reduce-scatter.11.cloned.1.call-update) | async-done | bytes 65552 | tf_op jit(solution)/shard_map/reduce_scatter | solution.py:84
  697.4 2.1 multiply_convert_fusion
  699.5 411.1 %reduce-scatter.7.cloned.1.call-done = f32[8,2048]{1,0:T(8,128)} async-done(((f32[512,2048]{1,0:T(8,128)}), f32[8,2048]{1,0:T(8,128)}) %reduce-scatter.7.cloned.1.call-update) | async-done | bytes 65552 | tf_op jit(solution)/shard_map/reduce_scatter | solution.py:59
  1110.6 2.1 multiply_convert_fusion.1
  (27 shorter events, 2.3 us)
Async XLA Ops:
  7.2 95.5 %copy-start = (bf16[2048,416]{0,1:T(8,128)(2,1)S(1)}, bf16[2048,416]{0,1:T(8,128)(2,1)}, u32[]{:S(2)}) copy-start(bf16[2048,416]{0,1:T(8,128)(2,1)} %param.7) | copy-start | bytes 5111812
  7.2 92.2 %all-gather.3.cloned.1.call-start = ((), (), s32[]{:S(2)}) async-start(), calls=%async_computation.4 | async-start | bytes 2129920 | tf_op jit(solution)/shard_map/all_gather | solution.py:32
  11.4 169.1 %all-gather.5.cloned.1.call-start = ((), (), s32[]{:S(2)}) async-start(), calls=%async_computation.7 | async-start | bytes 2129920 | tf_op jit(solution)/shard_map/all_gather | solution.py:69
  14.1 205.6 %reduce-scatter.5.cloned.1.call-start = ((), (), s32[]{:S(2)}) async-start(), calls=%async_computation.5 | async-start | bytes 2129920 | tf_op jit(solution)/shard_map/reduce_scatter | solution.py:35
  99.3 3.3 copy-start.4
  103.8 76.7 %copy-start.3 = (bf16[416,2048]{1,0:T(8,128)(2,1)S(1)}, bf16[416,2048]{1,0:T(8,128)(2,1)}, u32[]{:S(2)}) copy-start(bf16[416,2048]{1,0:T(8,128)(2,1)} %param.9) | copy-start | bytes 5111812
  105.1 146.3 %reduce-scatter.9.cloned.1.call-start = ((), (), s32[]{:S(2)}) async-start(), calls=%async_computation.8 | async-start | bytes 1064960 | tf_op jit(solution)/shard_map/reduce_scatter | solution.py:72
  184.0 513.3 %reduce-scatter.11.cloned.1.call-start = ((), (), s32[]{:S(2)}) async-start(), calls=%async_computation.9 | async-start | bytes 4259840 | tf_op jit(solution)/shard_map/reduce_scatter | solution.py:84
  279.5 1.5 copy-start.2
  284.3 826.2 %reduce-scatter.7.cloned.1.call-start = ((), (), s32[]{:S(2)}) async-start(), calls=%async_computation.6 | async-start | bytes 4259840 | tf_op jit(solution)/shard_map/reduce_scatter | solution.py:59
  303.7 5.2 copy-start.5
  407.9 3.7 copy-start.1
Sparse Core Ops, SparseCore 0:
  12.3 87.0 all-gather.2
  103.6 76.8 all-gather.4
  183.6 36.0 reduce-scatter.4
  222.6 28.6 reduce-scatter.8
  284.5 412.8 reduce-scatter.10
  699.8 410.7 reduce-scatter.6
where the time goes:
time: 1130 us; the launch traced here: 1120 us
  waiting for transfers between devices  918 us (81%)
  blocking collectives  118 us (10%)
  matrix products  30.9 us (3%)
  other arithmetic  27.1 us (2%)
  between operations  20.6 us (2%)
    reduce_scatter x1, waiting for transfers between devices, shards(): lax.psum_scatter(jnp.dot(rows, down_weight, preferred_element_type=jnp.fl...  411 us
    reduce_scatter x1, waiting for transfers between devices, shards(): lax.psum_scatter(contract_last(dg_all, gate_weight), 'hid', scatter_dimen...  281 us
    all_gather x1, waiting for transfers between devices, shards(): xq_all = lax.all_gather(xq, 'hid', axis=0, tiled=True)  85.2 us
    pmax x1, blocking collectives, shards(): grads_max = lax.pmax(jnp.stack([local_gu, local_down]), ('tok', 'hid'))  82.1 us
    all_gather x1, waiting for transfers between devices, shards(): grad_all = lax.all_gather(grad_q, 'hid', axis=0, tiled=True)  75.3 us
    reduce_scatter x1, waiting for transfers between devices, shards(): lax.psum_scatter(jnp.concatenate([jnp.dot(rows, gate_weight, preferred_el...  35.6 us
    reduce_scatter x1, waiting for transfers between devices, shards(): lax.psum_scatter(contract_last(rows, down_weight), 'tok', scatter_dimensi...  30 us
  transfers between devices with their start and end apart: 6, of which 6 were waited for; matrix products, arithmetic and copies ran while one was open for 4% of the time, Pallas kernels for 0%

commit v1 on v0

v1 whole, which is shorter than its diff:
```python
import jax
import jax.numpy as jnp
from jax import lax
from jax.experimental import pallas as pl
from jax.experimental.pallas import tpu as pltpu
from jax.sharding import PartitionSpec as P

MESH = pl.DeviceIdType.MESH
BF = jnp.bfloat16
F32 = jnp.float32
HALF = 1024
WIDE = 896
FILL = 512


def contract_last(left, right):
    return lax.dot_general(left, right, (((1,), (1,)), ((), ())), preferred_element_type=F32)


def contract_first(left, right):
    return lax.dot_general(left, right, (((0,), (0,)), ((), ())), preferred_element_type=F32)


def quantize(value, scale):
    return jnp.clip(value / scale, -448.0, 448.0).astype(BF)


class Links:
    def __init__(self, send, recv):
        self.send, self.recv, self.used, self.open = send, recv, 0, []

    def slots(self, count):
        first = self.used
        self.used += count
        return first

    def copy(self, src, dst, slot, device):
        return pltpu.make_async_remote_copy(
            src_ref=src,
            dst_ref=dst,
            send_sem=self.send.at[slot],
            recv_sem=self.recv.at[slot],
            device_id=device,
            device_id_type=MESH,
        )

    def start(self, src, dst, slot, device):
        copy = self.copy(src, dst, slot, device)
        copy.start()
        self.open.append(copy)

    def arrived(self, dst, slot, device):
        self.copy(dst, dst, slot, device).wait_recv()

    def finish(self):
        for copy in self.open:
            copy.wait_send()


N_SEMS = 160


def kernel(
    prior, tokens, out_grad, weights_hbm, down_hbm,
    out_ref, in_grad_ref, wide_hbm, wdown_hbm, peaks_ref,
    xb, gb, wide_w, down_w, swap_out, swap_in,
    part, keep, got1, send2, got2,
    dpart, dkeep, dgot1, dsend2, dgot2,
    hb, db,
    o_part, o_core, o_ring, o_send, o_got, o_zs, o_zr, o_fin, o_fr,
    i_part, i_core, i_ring, i_ring2, i_send, i_send2, i_got, i_got2, i_zs, i_zr, i_fin, i_fr,
    wide_g, down_g, max_s, max_r,
    send_sem, recv_sem, load_sem, store_sem,
):
    t = lax.axis_index("tok")
    h = lax.axis_index("hid")
    y, zh, x, c = h // 16, (h // 8) % 2, (h // 2) % 4, h % 2
    p, s = t % 2, t // 2

    def device(dt=0, dy=0, dz=0, dx=0, dc=0):
        hid = ((((y + dy) % 4) * 2 + (zh + dz) % 2) * 4 + (x + dx) % 4) * 2 + (c + dc) % 2
        return ((t + dt) % 4, hid)

    def beside():
        return (t + 1 - 2 * p, h)

    peers = [device(dx=d, dc=e) for d in range(4) for e in range(2) if d or e]
    peers += [device(dy=d) for d in (1, 2, 3)]
    peers += [device(dt=d, dz=e) for d in range(4) for e in range(2) if d or e]
    barrier = pltpu.get_barrier_semaphore()
    for peer in peers:
        pl.semaphore_signal(barrier, inc=1, device_id=peer, device_id_type=MESH)

    load_w = pltpu.make_async_copy(weights_hbm, wide_w, load_sem.at[0])
    load_w.start()
    load_d = pltpu.make_async_copy(down_hbm, down_w.at[pl.ds(0, 416)], load_sem.at[1])
    load_d.start()
    down_w[pl.ds(416, 96), :] = jnp.zeros((96, 2048), BF)

    s0, s1, s2, s3 = [prior[i] / 448.0 for i in range(4)]
    mine = pl.ds(pl.multiple_of(c * HALF, HALF), HALF)
    other = pl.ds(pl.multiple_of((1 - c) * HALF, HALF), HALF)

    tok_f = tokens[...].astype(F32)
    og_f = out_grad[...].astype(F32)
    max_x = jnp.max(jnp.abs(tok_f))
    max_g = jnp.max(jnp.abs(og_f))
    swap_out[pl.ds(0, 8), :] = quantize(tok_f, s0).astype(F32)
    swap_out[pl.ds(8, 8), :] = quantize(og_f, s2).astype(F32)

    links = Links(send_sem, recv_sem)
    core = device(dc=1)

    pl.semaphore_wait(barrier, len(peers))

    slot = links.slots(1)
    links.start(swap_out.at[:, other], swap_in, slot, core)
    links.arrived(swap_in, slot, core)
    own = swap_out[:, mine]
    theirs = swap_in[...]
    low = jnp.where(c == 0, own, theirs)
    high = jnp.where(c == 0, theirs, own)
    xb[y, zh, x, :, mine] = jnp.concatenate([low[0:8], high[0:8]], axis=0).astype(BF)
    gb[y, zh, x, :, mine] = jnp.concatenate([low[8:16], high[8:16]], axis=0).astype(BF)

    def step_x(d):
        return device(dx=d)

    def step_y(d):
        return device(dy=d)

    tx1, tx2, tz = links.slots(4), links.slots(4), links.slots(1)
    ty1, ty2, tc = links.slots(4), links.slots(4), links.slots(4)
    gy1, gy2, gz = links.slots(4), links.slots(4), links.slots(1)
    gx1, gx2, gc = links.slots(4), links.slots(4), links.slots(4)
    away = device(dz=1)
    xblock = xb.at[y, zh, x, :, mine]
    gblock = gb.at[y, zh, x, :, mine]
    links.start(xblock, xblock, tz, away)
    for d in (1, 3, 2):
        links.start(xblock, xblock, tx1 + d, step_x(d))
    links.start(gblock, gblock, gz, away)
    for d in (1, 3, 2):
        links.start(gblock, gblock, gy1 + d, step_y(d))
    xblock2 = xb.at[y, 1 - zh, x, :, mine]
    gblock2 = gb.at[y, 1 - zh, x, :, mine]
    links.arrived(xblock2, tz, away)
    for d in (1, 3, 2):
        links.start(xblock2, xblock2, tx2 + d, step_x(d))
    links.arrived(gblock2, gz, away)
    for d in (1, 3, 2):
        links.start(gblock2, gblock2, gy2 + d, step_y(d))
    for z, tx, ty, gy, gx in ((zh, tx1, ty1, gy1, gx1), (1 - zh, tx2, ty2, gy2, gx2)):
        for d in (1, 3, 2):
            links.arrived(xb.at[y, z, (x - d) % 4, :, mine], tx + d, step_x(4 - d))
        rows = xb.at[y, z, :, :, mine]
        for d in (1, 3, 2):
            links.start(rows, rows, ty + d, step_y(d))
        for d in (1, 3, 2):
            links.arrived(gb.at[(y - d) % 4, z, x, :, mine], gy + d, step_y(4 - d))
        rows = gb.at[:, z, x, :, mine]
        for d in (1, 3, 2):
            links.start(rows, rows, gx + d, step_x(d))
    rows = xb.at[y, :, :, :, mine]
    links.start(rows, rows, tc, core)
    rows = gb.at[:, :, x, :, mine]
    links.start(rows, rows, gc, core)

    load_w.wait()
    load_d.wait()

    order = ((1 - p) + 2 * (1 - s), (1 - p) + 2 * s, p + 2 * (1 - s), p + 2 * s)
    r1, r2 = links.slots(2), links.slots(1)
    d1, d2 = links.slots(2), links.slots(1)
    partner = beside()
    far = device(dt=2)
    gdone = (1, 3, 2, None)
    for j, k in enumerate(order):
        yk = (y + k) % 4
        rows = xb.at[yk, :, :, :, mine]

        @pl.when(k != 0)
        def _():
            for z, ty in ((zh, ty1), (1 - zh, ty2)):
                links.arrived(xb.at[yk, z, :, :, mine], ty + (4 - k), device(dy=k))
            links.copy(rows, rows, tc + k, core).start()

        g = gdone[j]
        if g is not None:
            for z, gx in ((zh, gx1), (1 - zh, gx2)):
                links.arrived(gb.at[:, z, (x + g) % 4, :, mine], gx + (4 - g), step_x(g))
            rows_g = gb.at[:, :, (x + g) % 4, :, mine]
            links.start(rows_g, rows_g, gc + g, core)
        links.arrived(xb.at[yk, :, :, :, other], tc + k, core)
        value = jnp.dot(
            xb[yk].reshape(128, 2048), wide_w[...], preferred_element_type=F32
        )
        if j < 2:
            part[j] = value.astype(BF)
            to = 1 - s if j == 0 else s
            links.start(part.at[j], got1.at[to], r1 + to, partner)
        else:
            keep[j - 2] = value
    for g in (0, 1, 3, 2):
        links.arrived(gb.at[:, :, (x + g) % 4, :, other], gc + g, core)
    for j, k in enumerate(order):
        yk = (y + k) % 4
        value = contract_last(gb[yk].reshape(128, 2048), down_w[...])
        if j < 2:
            dpart[j] = value.astype(BF)
            to = 1 - s if j == 0 else s
            links.start(dpart.at[j], dgot1.at[to], d1 + to, partner)
        else:
            dkeep[j - 2] = value
    links.arrived(got1.at[1 - s], r1 + (1 - s), partner)
    send2[...] = (keep[0] + got1[1 - s].astype(F32)).astype(BF)
    links.start(send2, got2, r2, far)
    links.arrived(dgot1.at[1 - s], d1 + (1 - s), partner)
    dsend2[...] = (dkeep[0] + dgot1[1 - s].astype(F32)).astype(BF)
    links.start(dsend2, dgot2, d2, far)

    lane = lax.broadcasted_iota(jnp.int32, (128, FILL), 1)
    inside = lane < 416
    yt = (y + t) % 4
    h1, h2, h3 = links.slots(1), links.slots(1), links.slots(1)
    g1, g2, g3 = links.slots(1), links.slots(1), links.slots(1)

    links.arrived(got1.at[s], r1 + s, partner)
    links.arrived(got2, r2, far)
    both = (keep[1] + got1[s].astype(F32) + got2[...].astype(F32)) * s0
    gate = jnp.where(inside, both[:, :FILL], 0.0)
    up = jnp.where(inside, pltpu.roll(both, WIDE - 416, 1)[:, :FILL], 0.0)
    sig = jax.nn.sigmoid(gate)
    act = gate * sig
    hidden = act * up
    max_h = jnp.max(jnp.abs(hidden))
    hb[yt] = quantize(hidden, s1)
    links.start(hb.at[yt], hb.at[yt], h1, far)
    links.start(hb.at[yt], hb.at[yt], h2, partner)

    links.arrived(dgot1.at[s], d1 + s, partner)
    links.arrived(dgot2, d2, far)
    dhidden = (dkeep[1] + dgot1[s].astype(F32) + dgot2[...].astype(F32)) * s2
    dgate = dhidden * up * sig * (1.0 + gate * (1.0 - sig))
    dup = dhidden * act
    max_p = jnp.maximum(jnp.max(jnp.abs(dgate)), jnp.max(jnp.abs(dup)))
    room = jnp.zeros((128, WIDE - FILL), F32)
    dgq = jnp.concatenate([quantize(dgate, s3).astype(F32), room], axis=1)
    duq = jnp.concatenate([quantize(dup, s3).astype(F32), room], axis=1)
    db[yt] = (dgq + pltpu.roll(duq, 416, 1)).astype(BF)
    links.start(db.at[yt], db.at[yt], g1, far)
    links.start(db.at[yt], db.at[yt], g2, partner)

    yf = (y + (t + 2) % 4) % 4
    yp = (y + partner[0]) % 4
    ypf = (y + (partner[0] + 2) % 4) % 4
    links.arrived(hb.at[yf], h1, far)
    links.start(hb.at[yf], hb.at[yf], h3, partner)

    o_cs, i_cs = links.slots(4), links.slots(4)

    def out_block(at, n):
        value = jnp.dot(hb[at], down_w[...], preferred_element_type=F32)
        o_part[at] = value.astype(BF).reshape(2, 4, 16, 2048)
        links.start(o_part.at[at, :, :, :, other], o_core.at[at], o_cs + n, core)

    def in_block(at, n):
        value = contract_last(db[at], wide_w[...])
        i_part[at] = value.astype(BF).reshape(2, 4, 16, 2048)
        links.start(i_part.at[at, :, :, :, other], i_core.at[at], i_cs + n, core)

    blocks = (yt, yf, yp, ypf)

    out_block(yt, 0)
    out_block(yf, 1)
    links.arrived(db.at[yf], g1, far)
    links.start(db.at[yf], db.at[yf], g3, partner)
    links.arrived(hb.at[yp], h2, partner)
    links.arrived(hb.at[ypf], h3, partner)
    out_block(yp, 2)
    out_block(ypf, 3)

    o_y, o_x, o_z, o_c = links.slots(4), links.slots(4), links.slots(1), links.slots(1)
    for n, at in enumerate(blocks):
        links.arrived(o_core.at[at], o_cs + n, core)
        value = o_part[at, :, :, :, mine].astype(F32) + o_core[at].astype(F32)
        o_core[at] = value.astype(BF)
    for d in (1, 3, 2):
        links.start(o_core.at[(y + d) % 4], o_ring.at[d - 1], o_y + d, step_y(d))

    flipped = hb[...].reshape(512, FILL).astype(F32).T.astype(BF)

    def down_tile(i, top):
        columns = pl.ds(pl.multiple_of(i * 256, 256), 256)
        rows = gb[:, :, :, :, columns].reshape(512, 256)
        value = jnp.dot(flipped, rows, preferred_element_type=F32)[:416] * (s1 * s2)
        down_g[:, columns] = value.astype(BF)
        return jnp.maximum(top, jnp.max(jnp.abs(value)))

    max_d = lax.fori_loop(0, 8, down_tile, jnp.float32(0.0))
    store_d = pltpu.make_async_copy(down_g, wdown_hbm, store_sem.at[0])
    store_d.start()

    in_block(yt, 0)
    in_block(yf, 1)

    for d in (1, 3, 2):
        links.arrived(o_ring.at[d - 1], o_y + d, step_y(4 - d))
    total = o_core[y].astype(F32)
    for d in (1, 2, 3):
        total = total + o_ring[d - 1].astype(F32)
    o_send[...] = total.astype(BF)
    for d in (1, 3, 2):
        links.start(o_send.at[:, (x + d) % 4], o_got.at[d - 1], o_x + d, step_x(d))

    links.arrived(db.at[yp], g2, partner)
    links.arrived(db.at[ypf], g3, partner)
    in_block(yp, 2)
    in_block(ypf, 3)

    def rest(links, send, got, x_slot, z_slot, zs, zr, device_of, index):
        for d in (1, 3, 2):
            links.arrived(got.at[d - 1], x_slot + d, device_of(4 - d))
        total = send[:, index].astype(F32) if len(send.shape) == 4 else None
        for d in (1, 2, 3):
            total = total + got[d - 1].astype(F32)
        zs[...] = total
        links.start(zs.at[1 - zh], zr, z_slot, away)

    rest(links, o_send, o_got, o_x, o_z, o_zs, o_zr, step_x, x)

    i_y, i_x, i_z, i_c = links.slots(4), links.slots(4), links.slots(1), links.slots(1)
    j_y, j_x, j_z = links.slots(4), links.slots(4), links.slots(1)
    for n, at in enumerate(blocks):
        links.arrived(i_core.at[at], i_cs + n, core)
        value = i_part[at, :, :, :, mine].astype(F32) + i_core[at].astype(F32)
        i_core[at] = value.astype(BF)
    left, right = pl.ds(0, 512), pl.ds(512, 512)
    for d in (1, 3, 2):
        links.start(
            i_core.at[(y + d) % 4, :, :, :, left], i_ring.at[d - 1], i_y + d, step_y(d)
        )
        links.start(
            i_core.at[:, :, (x + d) % 4, :, right], i_ring2.at[d - 1], j_x + d, step_x(d)
        )

    links.arrived(o_zr, o_z, away)
    o_fin[...] = o_zs[zh] + o_zr[...]
    rows_other = pl.ds(pl.multiple_of((1 - c) * 8, 8), 8)
    rows_mine = pl.ds(pl.multiple_of(c * 8, 8), 8)
    links.start(o_fin.at[rows_other], o_fr, o_c, core)

    def wide_tile(i, top):
        columns = pl.ds(pl.multiple_of(i * 256, 256), 256)
        rows = xb[:, :, :, :, columns].reshape(512, 256)
        value = contract_first(rows, db[...].reshape(512, WIDE)) * (s0 * s3)
        wide_g[columns, :] = value.astype(BF)
        return jnp.maximum(top, jnp.max(jnp.abs(value)))

    max_w = lax.fori_loop(0, 8, wide_tile, jnp.float32(0.0))
    store_w = pltpu.make_async_copy(wide_g, wide_hbm, store_sem.at[1])
    store_w.start()

    row = lax.broadcasted_iota(jnp.int32, (8, 128), 0)
    tops = jnp.zeros((8, 128), F32)
    for n, value in enumerate((max_x, max_h, max_g, max_p, max_w, max_d)):
        tops = jnp.where(row == n, value, tops)

    def send_tops(stage, value, offsets):
        first = links.slots(len(offsets))
        max_s[stage] = value
        for n, offset in enumerate(offsets):
            links.start(max_s.at[stage], max_r.at[stage, n], first + n, device(**offset))
        return first

    def take_tops(stage, value, offsets, first):
        for n, offset in enumerate(offsets):
            back = {name: -d for name, d in offset.items()}
            links.arrived(max_r.at[stage, n], first + n, device(**back))
            value = jnp.maximum(value, max_r[stage, n])
        return value

    plane = [dict(dx=d, dc=e) for d in range(4) for e in range(2) if d or e]
    depth = [dict(dt=d, dz=e) for d in range(4) for e in range(2) if d or e]
    column = [dict(dy=d) for d in (1, 2, 3)]
    first = send_tops(0, tops, plane)

    for d in (1, 3, 2):
        links.arrived(i_ring.at[d - 1], i_y + d, step_y(4 - d))
    total = i_core[y, :, :, :, left].astype(F32)
    for d in (1, 2, 3):
        total = total + i_ring[d - 1].astype(F32)
    i_send[...] = total.astype(BF)
    for d in (1, 3, 2):
        links.start(i_send.at[:, (x + d) % 4], i_got.at[d - 1], i_x + d, step_x(d))
    for d in (1, 3, 2):
        links.arrived(i_ring2.at[d - 1], j_x + d, step_x(4 - d))
    total = i_core[:, :, x, :, right].astype(F32)
    for d in (1, 2, 3):
        total = total + i_ring2[d - 1].astype(F32)
    i_send2[...] = total.astype(BF)
    for d in (1, 3, 2):
        links.start(i_send2.at[(y + d) % 4], i_got2.at[d - 1], j_y + d, step_y(d))

    tops = take_tops(0, tops, plane, first)
    first = send_tops(1, tops, column)

    for d in (1, 3, 2):
        links.arrived(i_got.at[d - 1], i_x + d, step_x(4 - d))
    total = i_send[:, x].astype(F32)
    for d in (1, 2, 3):
        total = total + i_got[d - 1].astype(F32)
    i_zs[:, :, left] = total
    for d in (1, 3, 2):
        links.arrived(i_got2.at[d - 1], j_y + d, step_y(4 - d))
    total = i_send2[y].astype(F32)
    for d in (1, 2, 3):
        total = total + i_got2[d - 1].astype(F32)
    i_zs[:, :, right] = total
    links.start(i_zs.at[1 - zh], i_zr, i_z, away)

    tops = take_tops(1, tops, column, first)
    first = send_tops(2, tops, depth)

    links.arrived(o_fr, o_c, core)
    out_ref[:, mine] = (o_fin[rows_mine, :] * s1).astype(BF)
    out_ref[:, other] = (o_fr[...] * s1).astype(BF)

    links.arrived(i_zr, i_z, away)
    i_fin[...] = i_zs[zh] + i_zr[...]
    links.start(i_fin.at[rows_other], i_fr, i_c, core)

    tops = take_tops(2, tops, depth, first)
    peaks_ref[pl.ds(0, 8), :] = tops
    peaks_ref[pl.ds(8, 8), :] = jnp.log(tops + 1e-6)

    links.arrived(i_fr, i_c, core)
    in_grad_ref[:, mine] = (i_fin[rows_mine, :] * s3).astype(BF)
    in_grad_ref[:, other] = (i_fr[...] * s3).astype(BF)

    for k in (1, 2, 3):
        rows = xb.at[0, :, :, :, mine]
        links.copy(rows, rows, tc + k, core).wait_send()
    links.finish()
    store_d.wait()
    store_w.wait()
    assert links.used <= N_SEMS


def shards(tokens, gate_weight, up_weight, down_weight, out_grad, amax_prior):
    width = gate_weight.shape[1]
    weights = jnp.concatenate(
        [gate_weight, up_weight, jnp.zeros((2048, WIDE - 2 * width), BF)], axis=1
    )
    vmem = pl.BlockSpec(memory_space=pltpu.VMEM)
    hbm = pl.BlockSpec(memory_space=pl.ANY)
    V = pltpu.VMEM
    output, input_grad, wide, wdown, peaks = pl.pallas_call(
        kernel,
        out_shape=(
            jax.ShapeDtypeStruct((8, 2048), BF),
            jax.ShapeDtypeStruct((8, 2048), BF),
            jax.ShapeDtypeStruct((2048, WIDE), BF),
            jax.ShapeDtypeStruct((416, 2048), BF),
            jax.ShapeDtypeStruct((16, 128), F32),
        ),
        in_specs=[pl.BlockSpec(memory_space=pltpu.SMEM), vmem, vmem, hbm, hbm],
        out_specs=(vmem, vmem, hbm, hbm, vmem),
        scratch_shapes=[
            V((4, 2, 4, 16, 2048), BF), V((4, 2, 4, 16, 2048), BF),
            V((2048, WIDE), BF), V((FILL, 2048), BF),
            V((16, 2048), F32), V((16, HALF), F32),
            V((2, 128, WIDE), BF), V((2, 128, WIDE), F32), V((2, 128, WIDE), BF),
            V((128, WIDE), BF), V((128, WIDE), BF),
            V((2, 128, FILL), BF), V((2, 128, FILL), F32), V((2, 128, FILL), BF),
            V((128, FILL), BF), V((128, FILL), BF),
            V((4, 128, FILL), BF), V((4, 128, WIDE), BF),
            V((4, 2, 4, 16, 2048), BF), V((4, 2, 4, 16, HALF), BF), V((3, 2, 4, 16, HALF), BF),
            V((2, 4, 16, HALF), BF), V((3, 2, 16, HALF), BF),
            V((2, 16, HALF), F32), V((16, HALF), F32), V((16, HALF), F32), V((8, HALF), F32),
            V((4, 2, 4, 16, 2048), BF), V((4, 2, 4, 16, HALF), BF),
            V((3, 2, 4, 16, 512), BF), V((3, 4, 2, 16, 512), BF),
            V((2, 4, 16, 512), BF), V((4, 2, 16, 512), BF),
            V((3, 2, 16, 512), BF), V((3, 2, 16, 512), BF),
            V((2, 16, HALF), F32), V((16, HALF), F32), V((16, HALF), F32), V((8, HALF), F32),
            V((2048, WIDE), BF), V((416, 2048), BF),
            V((3, 8, 128), F32), V((3, 7, 8, 128), F32),
            pltpu.SemaphoreType.DMA((N_SEMS,)), pltpu.SemaphoreType.DMA((N_SEMS,)),
            pltpu.SemaphoreType.DMA((2,)), pltpu.SemaphoreType.DMA((2,)),
        ],
        compiler_params=pltpu.CompilerParams(
            collective_id=0, has_side_effects=True, vmem_limit_bytes=60 << 20
        ),
        name="layer",
    )(amax_prior, tokens, out_grad, weights, down_weight)
    wide_top = peaks[4, 0] + 1e-6
    down_top = peaks[5, 0] + 1e-6
    gate_grad = (wide[:, :width].astype(F32) / wide_top).astype(BF)
    up_grad = (wide[:, width : 2 * width].astype(F32) / wide_top).astype(BF)
    down_grad = (wdown.astype(F32) / down_top).astype(BF)
    return (output, input_grad, gate_grad, up_grad, down_grad, peaks[8:14, 0])


def solution(mesh):
    placed = (
        P("hid", "tok"),
        P("tok", "hid"),
        P("tok", "hid"),
        P("hid", "tok"),
        P("hid", "tok"),
        P(),
    )
    return jax.shard_map(
        shards,
        mesh=mesh,
        in_specs=placed,
        out_specs=(
            P("hid", "tok"),
            P("hid", "tok"),
            P("tok", "hid"),
            P("tok", "hid"),
            P("hid", "tok"),
            P(),
        ),
        check_vma=False,
    )
```

time: 1130 us -> 157 us (0.14)
  waiting for transfers between devices: 918 us -> 0 us
  Pallas kernels: 0 us -> 125 us
  blocking collectives: 118 us -> 0 us
  matrix products: 30.9 us -> 0 us
  between operations: 20.6 us -> 1.96 us
  other arithmetic: 27.1 us -> 12.8 us
  local copies, waits for them, and re-layouts: 4.12 us -> 16.5 us
    reduce_scatter x4 -> x0, waiting for transfers between devices: 758 us -> none  [the longest x1 411 us: shards(): lax.psum_scatter(jnp.dot(rows, down_weight, preferred_element_type=jnp.fl...]
    all_gather x2 -> x0, waiting for transfers between devices: 161 us -> none  [the longest x1 85.2 us: shards(): xq_all = lax.all_gather(xq, 'hid', axis=0, tiled=True)]
    pallas_call x0 -> x1, Pallas kernels: none -> 125 us  [shards(): pl.pallas_call(kernel, out_shape=(jax.ShapeDtypeStruct((8, 2048), BF), ja...]
    pmax x1 -> x0, blocking collectives: 82.1 us -> none  [shards(): grads_max = lax.pmax(jnp.stack([local_gu, local_down]), ('tok', 'hid'))]
    all_gather x3 -> x0, blocking collectives: 36 us -> none  [the longest x1 12.7 us: shards(): lax.all_gather(duq, 'tok', axis=0, tiled=True)]
    dot_general x9 -> x0, matrix products: 30.9 us -> none  [the longest x3 13.7 us: contract_first(): lax.dot_general(left, right, (((0,), (0,)), ((), ())), preferred_element_...]
    unnamed x12 -> x10, local copies, waits for them, and re-layouts: 0.2 us -> 13.9 us
  transfers between devices with their start and end apart: 6 -> 0, of which waited for: 6 -> 0; matrix products, arithmetic and copies ran while one was open for 4% -> 0% of each run, Pallas kernels for 0% -> 0%
where the time goes in v1:
time: 157 us; the launch traced here: 156 us
  Pallas kernels  125 us (80%)
  local copies, waits for them, and re-layouts  16.5 us (11%)
  other arithmetic  12.8 us (8%)
  between operations  1.96 us (1%)
    pallas_call x1, Pallas kernels, shards(): pl.pallas_call(kernel, out_shape=(jax.ShapeDtypeStruct((8, 2048), BF), ja...  125 us
    unnamed x10, local copies, waits for them, and re-layouts  13.9 us
    concatenate x1, other arithmetic, shards(): jnp.concatenate([gate_weight, up_weight, jnp.zeros((2048, WIDE - 2 * widt...  5.04 us
    convert_element_type x1, other arithmetic, shards(): up_grad = (wide[:, width:2 * width].astype(F32) / wide_top).astype(BF)  4.72 us

profile of v1, /device:TPU:1, one launch (start us, length us, event | category | flops | bytes accessed | tf_op | source)
XLA Modules:
  0.0 156.4 jit_solution(16459031777502118828)
XLA Ops:
  0.6 0.1 pad.2.clone
  0.7 2.8 %copy.16 = bf16[2048,416]{1,0:T(8,128)(2,1)S(1)} copy(bf16[2048,416]{0,1:T(8,128)(2,1)} %param.7) | data formatting | bytes 3407872 | tf_op args[1]
  3.5 3.8 %copy.17 = bf16[2048,416]{1,0:T(8,128)(2,1)} copy(bf16[2048,416]{0,1:T(8,128)(2,1)} %param.8) | data formatting | bytes 3407872 | tf_op args[2]
  7.3 5.0 %maximum_maximum_fusion.weights_hbm = bf16[2048,896]{1,0:T(8,128)(2,1)} fusion(bf16[2048,416]{1,0:T(8,128)(2,1)} %copy.17, bf16[2048,416]{1,0:T(8,128)(2,1)S(1)} %copy.16, bf16[896]{0:T(1024)(128)(2,1)S(1)} %pad.2.clone), kind=kLoop, calls=%fused_computation.2 | loop fusion | flops 11010048 | bytes 7079680 | tf_op jit(solution)/shard_map/concatenate | solution.py:452
  12.4 125.1 %layer.1 = (bf16[8,2048]{1,0:T(8,128)(2,1)}, bf16[8,2048]{1,0:T(8,128)(2,1)}, bf16[2048,896]{1,0:T(8,128)(2,1)}, bf16[416,2048]{1,0:T(8,128)(2,1)}, f32[16,128]{1,0:T(8,128)}) custom-call(f32[4]{0:T(128)} %prior.1, bf16[8,2048]{1,0:T(8,128)(2,1)} %tokens.1, bf16[8,2048]{1,0:T(8,128)(2,1)} %out_grad.1, bf16[2048,896]{1,0:T(8,128)(2,1)} %maximum_maximum_fusion.weights_hbm, ...), custom_call_target="tpu_custom_call" | custom-call | tf_op jit(solution)/shard_map/layer/pallas_call | solution.py:458
  137.4 1.3 slice_reduce_fusion
  138.7 1.3 fusion
  141.3 3.0 %divide_convert_fusion.2 = bf16[416,2048]{1,0:T(8,128)(2,1)} fusion(bf16[416,2048]{1,0:T(8,128)(2,1)} %get-tuple-element.15, f32[]{:T(128)} %bitcast.1), kind=kLoop, calls=%fused_computation.3 | loop fusion | flops 2555904 | bytes 3407876 | tf_op jit(solution)/shard_map/convert_element_type | solution.py:500
  144.3 4.7 %divide_convert_fusion = (bf16[2048,416]{1,0:T(8,128)(2,1)}, bf16[2048,416]{1,0:T(8,128)(2,1)S(1)}) fusion(bf16[2048,896]{1,0:T(8,128)(2,1)} %get-tuple-element.13, f32[]{:T(128)} %bitcast), kind=kLoop, calls=%fused_computation | loop fusion | flops 5111808 | bytes 6815748 | tf_op jit(solution)/shard_map/convert_element_type | solution.py:499
  149.1 0.0 copy-start.1
  149.1 0.0 copy-start
  149.1 3.8 %copy.19 = bf16[2048,416]{0,1:T(8,128)(2,1)} copy(bf16[2048,416]{1,0:T(8,128)(2,1)} %get-tuple-element.28) | data formatting | bytes 3407872
  152.9 2.2 %copy.18 = bf16[2048,416]{0,1:T(8,128)(2,1)} copy(bf16[2048,416]{1,0:T(8,128)(2,1)S(1)} %get-tuple-element.29) | data formatting | bytes 3407872
  155.1 0.0 copy-done.1
  155.1 0.6 copy.22
  155.7 0.0 copy-done
  155.7 0.6 copy.23
  (1 shorter events, 0.0 us)
Async XLA Ops:
  149.1 6.1 %copy-start.1 = (bf16[8,2048]{1,0:T(8,128)(2,1)S(1)}, bf16[8,2048]{1,0:T(8,128)(2,1)}, u32[]{:S(2)}) copy-start(bf16[8,2048]{1,0:T(8,128)(2,1)} %get-tuple-element.38) | copy-start | bytes 98308
  149.1 6.7 %copy-start = (bf16[8,2048]{1,0:T(8,128)(2,1)S(1)}, bf16[8,2048]{1,0:T(8,128)(2,1)}, u32[]{:S(2)}) copy-start(bf16[8,2048]{1,0:T(8,128)(2,1)} %get-tuple-element.39) | copy-start | bytes 98308

commit v2 on v1

v2 whole, which is shorter than its diff:
```python
import jax
import jax.numpy as jnp
from jax import lax
from jax.experimental import pallas as pl
from jax.experimental.pallas import tpu as pltpu
from jax.sharding import PartitionSpec as P

MESH = pl.DeviceIdType.MESH
BF = jnp.bfloat16
F32 = jnp.float32
HALF = 1024
UNITS = 416
WIDE = 832


def contract_last(left, right):
    return lax.dot_general(left, right, (((1,), (1,)), ((), ())), preferred_element_type=F32)


def contract_first(left, right):
    return lax.dot_general(left, right, (((0,), (0,)), ((), ())), preferred_element_type=F32)


def quantize(value, scale):
    return jnp.clip(value / scale, -448.0, 448.0).astype(BF)


class Links:
    def __init__(self, send, recv):
        self.send, self.recv, self.used, self.open = send, recv, 0, []

    def slots(self, count):
        first = self.used
        self.used += count
        return first

    def copy(self, src, dst, slot, device):
        return pltpu.make_async_remote_copy(
            src_ref=src,
            dst_ref=dst,
            send_sem=self.send.at[slot],
            recv_sem=self.recv.at[slot],
            device_id=device,
            device_id_type=MESH,
        )

    def start(self, src, dst, slot, device):
        copy = self.copy(src, dst, slot, device)
        copy.start()
        self.open.append(copy)

    def arrived(self, dst, slot, device):
        self.copy(dst, dst, slot, device).wait_recv()

    def finish(self):
        for copy in self.open:
            copy.wait_send()


N_SEMS = 240


def kernel(
    prior, tokens, out_grad, gate_hbm, up_hbm, down_hbm,
    out_ref, in_grad_ref, wide_hbm, wdown_hbm, peaks_ref,
    xb, gb, wide_w, down_w, swap_out, swap_in,
    part, keep, got1, send2, got2,
    dpart, dkeep, dgot1, dsend2, dgot2,
    hb, db,
    o_refs, i_refs,
    wide_g, down_g, max_s, max_r,
    send_sem, recv_sem, load_sem, store_sem,
):
    t = lax.axis_index("tok")
    h = lax.axis_index("hid")
    y, zh, x, c = h // 16, (h // 8) % 2, (h // 2) % 4, h % 2
    p, s = t % 2, t // 2

    def device(dt=0, dy=0, dz=0, dx=0, dc=0):
        hid = ((((y + dy) % 4) * 2 + (zh + dz) % 2) * 4 + (x + dx) % 4) * 2 + (c + dc) % 2
        return ((t + dt) % 4, hid)

    def beside():
        return (t + 1 - 2 * p, h)

    peers = [device(dx=d, dc=e) for d in range(4) for e in range(2) if d or e]
    peers += [device(dy=d) for d in (1, 2, 3)]
    peers += [device(dt=d, dz=e) for d in range(4) for e in range(2) if d or e]
    barrier = pltpu.get_barrier_semaphore()
    for peer in peers:
        pl.semaphore_signal(barrier, inc=1, device_id=peer, device_id_type=MESH)

    loads = [
        pltpu.make_async_copy(gate_hbm, wide_w.at[pl.ds(0, UNITS)], load_sem.at[0]),
        pltpu.make_async_copy(up_hbm, wide_w.at[pl.ds(UNITS, UNITS)], load_sem.at[1]),
        pltpu.make_async_copy(down_hbm, down_w, load_sem.at[2]),
    ]
    for load in loads:
        load.start()

    s0, s1, s2, s3 = [prior[i] / 448.0 for i in range(4)]
    mine = pl.ds(pl.multiple_of(c * HALF, HALF), HALF)
    other = pl.ds(pl.multiple_of((1 - c) * HALF, HALF), HALF)

    tok_f = tokens[...].astype(F32)
    og_f = out_grad[...].astype(F32)
    max_x = jnp.max(jnp.abs(tok_f))
    max_g = jnp.max(jnp.abs(og_f))
    swap_out[pl.ds(0, 8), :] = quantize(tok_f, s0).astype(F32)
    swap_out[pl.ds(8, 8), :] = quantize(og_f, s2).astype(F32)

    links = Links(send_sem, recv_sem)
    core = device(dc=1)

    pl.semaphore_wait(barrier, len(peers))

    slot = links.slots(1)
    links.start(swap_out.at[:, other], swap_in, slot, core)
    links.arrived(swap_in, slot, core)
    own = swap_out[:, mine]
    theirs = swap_in[...]
    low = jnp.where(c == 0, own, theirs)
    high = jnp.where(c == 0, theirs, own)
    xb[y, zh, x, :, mine] = jnp.concatenate([low[0:8], high[0:8]], axis=0).astype(BF)
    gb[y, zh, x, :, mine] = jnp.concatenate([low[8:16], high[8:16]], axis=0).astype(BF)

    def step_x(d):
        return device(dx=d)

    def step_y(d):
        return device(dy=d)

    away = device(dz=1)
    cols_xy = pl.ds(pl.multiple_of(c * HALF, 512), 512)
    cols_yx = pl.ds(pl.multiple_of(c * HALF + 512, 512), 512)

    class Gather:
        def __init__(self, buf):
            self.buf = buf
            self.z = links.slots(1)
            self.first = {a: (links.slots(4), links.slots(4)) for a in (0, 1)}
            self.second = {a: (links.slots(4), links.slots(4)) for a in (0, 1)}
            self.swap = (links.slots(4), links.slots(4))

        def level(self, a):
            return zh if a == 0 else 1 - zh

        def send_z(self):
            block = self.buf.at[y, zh, x, :, mine]
            links.start(block, block, self.z, away)

        def wait_z(self):
            links.arrived(self.buf.at[y, 1 - zh, x, :, mine], self.z, away)

        def send_first(self, a):
            z = self.level(a)
            for d in (1, 3, 2):
                block = self.buf.at[y, z, x, :, cols_xy]
                links.start(block, block, self.first[a][0] + d, step_x(d))
                block = self.buf.at[y, z, x, :, cols_yx]
                links.start(block, block, self.first[a][1] + d, step_y(d))

        def wait_first(self, a):
            z = self.level(a)
            for d in (1, 3, 2):
                block = self.buf.at[y, z, (x - d) % 4, :, cols_xy]
                links.arrived(block, self.first[a][0] + d, step_x(4 - d))
                block = self.buf.at[(y - d) % 4, z, x, :, cols_yx]
                links.arrived(block, self.first[a][1] + d, step_y(4 - d))

        def send_second(self, a):
            z = self.level(a)
            for d in (1, 3, 2):
                rows = self.buf.at[y, z, :, :, cols_xy]
                links.start(rows, rows, self.second[a][0] + d, step_y(d))
                rows = self.buf.at[:, z, x, :, cols_yx]
                links.start(rows, rows, self.second[a][1] + d, step_x(d))

        def wait_second(self, d):
            for a in (0, 1):
                z = self.level(a)
                rows = self.buf.at[(y - d) % 4, z, :, :, cols_xy]
                links.arrived(rows, self.second[a][0] + d, step_y(4 - d))
                rows = self.buf.at[:, z, (x - d) % 4, :, cols_yx]
                links.arrived(rows, self.second[a][1] + d, step_x(4 - d))

        def send_swap(self, d):
            rows = self.buf.at[(y - d) % 4, :, :, :, cols_xy]
            links.start(rows, rows, self.swap[0] + d, core)
            rows = self.buf.at[:, :, (x - d) % 4, :, cols_yx]
            links.start(rows, rows, self.swap[1] + d, core)

        def wait_swap(self):
            there_xy = pl.ds(pl.multiple_of((1 - c) * HALF, 512), 512)
            there_yx = pl.ds(pl.multiple_of((1 - c) * HALF + 512, 512), 512)
            for d in (0, 1, 3, 2):
                rows = self.buf.at[(y - d) % 4, :, :, :, there_xy]
                links.arrived(rows, self.swap[0] + d, core)
                rows = self.buf.at[:, :, (x - d) % 4, :, there_yx]
                links.arrived(rows, self.swap[1] + d, core)

    gx, gg = Gather(xb), Gather(gb)
    gx.send_z()
    gx.send_first(0)
    gg.send_z()
    gg.send_first(0)
    gx.wait_z()
    gx.send_first(1)
    gg.wait_z()
    gg.send_first(1)
    for gather in (gx, gg):
        gather.wait_first(0)
        gather.send_second(0)
        gather.wait_first(1)
        gather.send_second(1)
        gather.send_swap(0)
    for load in loads:
        load.wait()
    for d in (1, 3, 2):
        gx.wait_second(d)
        gx.send_swap(d)
    gx.wait_swap()

    order = ((1 - p) + 2 * (1 - s), (1 - p) + 2 * s, p + 2 * (1 - s), p + 2 * s)
    r1, r2 = links.slots(4), links.slots(2)
    d1, d2 = links.slots(2), links.slots(1)
    partner = beside()
    far = device(dt=2)
    units = (pl.ds(0, UNITS), pl.ds(UNITS, UNITS))

    def pair(buf, j):
        two = [buf[(y + k) % 4].reshape(128, 2048) for k in order[j : j + 2]]
        return jnp.concatenate(two, axis=0)

    value = contract_last(wide_w[...], pair(xb, 0))
    for j, to in ((0, 1 - s), (1, s)):
        part[j] = value[:, 128 * j : 128 * j + 128].astype(BF)
        for u in (0, 1):
            links.start(part.at[j, units[u]], got1.at[to, units[u]], r1 + 2 * to + u, partner)
    value = contract_last(wide_w[...], pair(xb, 2))
    keep[0] = value[:, :128]
    keep[1] = value[:, 128:]
    for d in (1, 3, 2):
        gg.wait_second(d)
        gg.send_swap(d)
    gg.wait_swap()
    value = contract_last(down_w[...], pair(gb, 0))
    for j, to in ((0, 1 - s), (1, s)):
        dpart[j] = value[:, 128 * j : 128 * j + 128].astype(BF)
        links.start(dpart.at[j], dgot1.at[to], d1 + to, partner)
    value = contract_last(down_w[...], pair(gb, 2))
    dkeep[0] = value[:, :128]
    dkeep[1] = value[:, 128:]
    for u in (0, 1):
        links.arrived(got1.at[1 - s, units[u]], r1 + 2 * (1 - s) + u, partner)
        send2[units[u], :] = (keep[0, units[u]] + got1[1 - s, units[u]].astype(F32)).astype(BF)
        links.start(send2.at[units[u]], got2.at[units[u]], r2 + u, far)
    links.arrived(dgot1.at[1 - s], d1 + (1 - s), partner)
    dsend2[...] = (dkeep[0] + dgot1[1 - s].astype(F32)).astype(BF)
    links.start(dsend2, dgot2, d2, far)
    yt = (y + t) % 4
    h1, h2, h3 = links.slots(1), links.slots(1), links.slots(1)
    g1, g2, g3 = links.slots(2), links.slots(2), links.slots(2)

    for u in (0, 1):
        links.arrived(got1.at[s, units[u]], r1 + 2 * s + u, partner)
        links.arrived(got2.at[units[u]], r2 + u, far)
    both = (keep[1] + got1[s].astype(F32) + got2[...].astype(F32)) * s0
    gate = both[:UNITS]
    up = both[UNITS:]
    sig = jax.nn.sigmoid(gate)
    act = gate * sig
    hidden = act * up
    max_h = jnp.max(jnp.abs(hidden))
    hb[yt] = quantize(hidden, s1)
    links.start(hb.at[yt], hb.at[yt], h1, far)
    links.start(hb.at[yt], hb.at[yt], h2, partner)

    links.arrived(dgot1.at[s], d1 + s, partner)
    links.arrived(dgot2, d2, far)
    dhidden = (dkeep[1] + dgot1[s].astype(F32) + dgot2[...].astype(F32)) * s2
    dgate = dhidden * up * sig * (1.0 + gate * (1.0 - sig))
    dup = dhidden * act
    max_p = jnp.maximum(jnp.max(jnp.abs(dgate)), jnp.max(jnp.abs(dup)))
    for u, value in ((0, dgate), (1, dup)):
        db[yt, units[u]] = quantize(value, s3)
        links.start(db.at[yt, units[u]], db.at[yt, units[u]], g1 + u, far)
    for u in (0, 1):
        links.start(db.at[yt, units[u]], db.at[yt, units[u]], g2 + u, partner)
    yf = (y + (t + 2) % 4) % 4
    yp = (y + partner[0]) % 4
    ypf = (y + (partner[0] + 2) % 4) % 4
    links.arrived(hb.at[yf], h1, far)
    links.start(hb.at[yf], hb.at[yf], h3, partner)

    class Spread:
        def __init__(self, part, core_in, ring_y, ring_x, then_x, then_y, got_x, got_y, zs, zr, fin, fr):
            self.part, self.core_in, self.ring_y, self.ring_x = part, core_in, ring_y, ring_x
            self.then_x, self.then_y, self.got_x, self.got_y = then_x, then_y, got_x, got_y
            self.zs, self.zr, self.fin, self.fr = zs, zr, fin, fr
            self.cores, self.yx, self.xy = links.slots(4), links.slots(4), links.slots(16)
            self.x, self.y, self.z, self.c = links.slots(4), links.slots(4), links.slots(1), links.slots(1)

        def block(self, n, left, right):
            value = contract_first(left, right)
            at = blocks[n]
            self.part[at] = value.astype(BF).reshape(2, 4, 16, 2048)
            links.start(self.part.at[at, :, :, :, other], self.core_in.at[at], self.cores + n, core)

        def first(self, n):
            at, d = blocks[n], steps[n]
            links.arrived(self.core_in.at[at], self.cores + n, core)
            value = self.part[at, :, :, :, mine].astype(F32) + self.core_in[at].astype(F32)
            self.core_in[at] = value.astype(BF)

            @pl.when(d != 0)
            def _():
                src = self.core_in.at[at, :, :, :, left]
                links.copy(src, self.ring_y.at[d - 1], self.yx + d, device(dy=d)).start()

            for e in (1, 3, 2):
                src = self.core_in.at[at, :, (x + e) % 4, :, right]
                links.start(src, self.ring_x.at[e - 1, at], self.xy + 4 * n + e, step_x(e))

        def second(self):
            for d in (1, 3, 2):
                links.arrived(self.ring_y.at[d - 1], self.yx + d, step_y(4 - d))
            total = self.core_in[y, :, :, :, left].astype(F32)
            for d in (1, 2, 3):
                total = total + self.ring_y[d - 1].astype(F32)
            self.then_x[...] = total.astype(BF)
            for d in (1, 3, 2):
                links.start(self.then_x.at[:, (x + d) % 4], self.got_x.at[d - 1], self.x + d, step_x(d))
            for n in range(4):
                for e in (1, 3, 2):
                    links.arrived(self.ring_x.at[e - 1, blocks[n]], self.xy + 4 * n + e, step_x(4 - e))
            total = self.core_in[:, :, x, :, right].astype(F32)
            for d in (1, 2, 3):
                total = total + self.ring_x[d - 1].astype(F32)
            self.then_y[...] = total.astype(BF)
            for d in (1, 3, 2):
                links.start(self.then_y.at[(y + d) % 4], self.got_y.at[d - 1], self.y + d, step_y(d))

        def third(self):
            for d in (1, 3, 2):
                links.arrived(self.got_x.at[d - 1], self.x + d, step_x(4 - d))
            total = self.then_x[:, x].astype(F32)
            for d in (1, 2, 3):
                total = total + self.got_x[d - 1].astype(F32)
            self.zs[:, :, left] = total
            for d in (1, 3, 2):
                links.arrived(self.got_y.at[d - 1], self.y + d, step_y(4 - d))
            total = self.then_y[y].astype(F32)
            for d in (1, 2, 3):
                total = total + self.got_y[d - 1].astype(F32)
            self.zs[:, :, right] = total
            links.start(self.zs.at[1 - zh], self.zr, self.z, away)

        def fourth(self):
            links.arrived(self.zr, self.z, away)
            self.fin[...] = self.zs[zh] + self.zr[...]
            links.start(self.fin.at[rows_other], self.fr, self.c, core)

        def last(self, ref, scale):
            links.arrived(self.fr, self.c, core)
            ref[:, mine] = (self.fin[rows_mine, :] * scale).astype(BF)
            ref[:, other] = (self.fr[...] * scale).astype(BF)

        def finish(self):
            for d in (1, 2, 3):
                src = self.core_in.at[0, :, :, :, left]
                links.copy(src, self.ring_y.at[0], self.yx + d, step_y(d)).wait_send()

    left, right = pl.ds(0, 512), pl.ds(512, 512)
    rows_other = pl.ds(pl.multiple_of((1 - c) * 8, 8), 8)
    rows_mine = pl.ds(pl.multiple_of(c * 8, 8), 8)
    steps = (t, (t + 2) % 4, partner[0], (partner[0] + 2) % 4)
    blocks = (yt, yf, yp, ypf)
    out_sum = Spread(*o_refs)
    in_sum = Spread(*i_refs)

    for n in (0, 1):
        out_sum.block(n, hb[blocks[n]], down_w[...])
    links.arrived(hb.at[yp], h2, partner)
    out_sum.block(2, hb[yp], down_w[...])
    links.arrived(hb.at[ypf], h3, partner)
    out_sum.block(3, hb[ypf], down_w[...])
    for n in range(4):
        out_sum.first(n)

    def pass_on():
        for u in (0, 1):
            links.arrived(db.at[yf, units[u]], g1 + u, far)
            links.start(db.at[yf, units[u]], db.at[yf, units[u]], g3 + u, partner)

    hq_all = jnp.concatenate([hb[n] for n in range(4)], axis=1)

    def down_tile(i, top):
        columns = pl.ds(pl.multiple_of(i * 256, 256), 256)
        rows = gb[:, :, :, :, columns].reshape(512, 256)
        value = jnp.dot(hq_all, rows, preferred_element_type=F32) * (s1 * s2)
        down_g[:, columns] = value.astype(BF)
        return jnp.maximum(top, jnp.max(jnp.abs(value)))

    max_d = lax.fori_loop(0, 4, down_tile, jnp.float32(0.0))
    pass_on()
    in_sum.block(0, db[yt], wide_w[...])
    in_sum.block(1, db[yf], wide_w[...])
    out_sum.second()
    max_d = lax.fori_loop(4, 8, down_tile, max_d)
    store_d = pltpu.make_async_copy(down_g, wdown_hbm, store_sem.at[0])
    store_d.start()
    in_sum.first(0)
    in_sum.first(1)
    for u in (0, 1):
        links.arrived(db.at[yp, units[u]], g2 + u, partner)
    in_sum.block(2, db[yp], wide_w[...])
    out_sum.third()
    for u in (0, 1):
        links.arrived(db.at[ypf, units[u]], g3 + u, partner)
    in_sum.block(3, db[ypf], wide_w[...])

    dq_all = jnp.concatenate([db[n] for n in range(4)], axis=1)

    def wide_tile(i, top):
        columns = pl.ds(pl.multiple_of(i * 256, 256), 256)
        rows = xb[:, :, :, :, columns].reshape(512, 256)
        value = jnp.dot(dq_all, rows, preferred_element_type=F32) * (s0 * s3)
        wide_g[:, columns] = value.astype(BF)
        return jnp.maximum(top, jnp.max(jnp.abs(value)))

    in_sum.first(2)
    max_w = lax.fori_loop(0, 2, wide_tile, jnp.float32(0.0))
    in_sum.first(3)
    max_w = lax.fori_loop(2, 8, wide_tile, max_w)
    store_w = pltpu.make_async_copy(wide_g, wide_hbm, store_sem.at[1])
    store_w.start()

    row = lax.broadcasted_iota(jnp.int32, (8, 128), 0)
    tops = jnp.zeros((8, 128), F32)
    for n, value in enumerate((max_x, max_h, max_g, max_p, max_w, max_d)):
        tops = jnp.where(row == n, value, tops)

    def send_tops(stage, value, offsets):
        first = links.slots(len(offsets))
        max_s[stage] = value
        for n, offset in enumerate(offsets):
            links.start(max_s.at[stage], max_r.at[stage, n], first + n, device(**offset))
        return first

    def take_tops(stage, value, offsets, first):
        for n, offset in enumerate(offsets):
            back = {name: -d for name, d in offset.items()}
            links.arrived(max_r.at[stage, n], first + n, device(**back))
            value = jnp.maximum(value, max_r[stage, n])
        return value

    plane = [dict(dx=d, dc=e) for d in range(4) for e in range(2) if d or e]
    depth = [dict(dt=d, dz=e) for d in range(4) for e in range(2) if d or e]
    column = [dict(dy=d) for d in (1, 2, 3)]
    first = send_tops(0, tops, plane)
    in_sum.second()
    tops = take_tops(0, tops, plane, first)
    first = send_tops(1, tops, column)
    out_sum.fourth()
    in_sum.third()
    tops = take_tops(1, tops, column, first)
    first = send_tops(2, tops, depth)
    out_sum.last(out_ref, s1)
    in_sum.fourth()
    tops = take_tops(2, tops, depth, first)
    peaks_ref[pl.ds(0, 8), :] = tops
    peaks_ref[pl.ds(8, 8), :] = jnp.log(tops + 1e-6)
    in_sum.last(in_grad_ref, s3)

    out_sum.finish()
    in_sum.finish()
    links.finish()
    store_d.wait()
    store_w.wait()
    assert links.used <= N_SEMS


def scale_grads(
    peaks, out_in, in_grad_in, wide_hbm, wdown_hbm,
    gate_out, up_out, down_out, out_ref, in_grad_ref, amaxes_ref,
    held, scaled, load_sem, store_sem,
):
    size = UNITS // 2
    halves = [pl.ds(n * size, size) for n in range(4)]
    sources = [wide_hbm.at[rows] for rows in halves] + [wdown_hbm.at[rows] for rows in halves[:2]]
    targets = [ref.at[rows] for ref in (gate_out, up_out, down_out) for rows in halves[:2]]
    loads = [
        pltpu.make_async_copy(source, held.at[n], load_sem.at[n]) for n, source in enumerate(sources)
    ]
    stores = [
        pltpu.make_async_copy(scaled.at[n], target, store_sem.at[n])
        for n, target in enumerate(targets)
    ]
    for load in loads:
        load.start()
    for n in range(6):
        amaxes_ref[n] = peaks[8 + n, 0]
    out_ref[...] = out_in[...]
    in_grad_ref[...] = in_grad_in[...]
    over_wide = 1.0 / (peaks[4, 0] + 1e-6)
    over_down = 1.0 / (peaks[5, 0] + 1e-6)
    for n in range(6):
        loads[n].wait()
        over = over_wide if n < 4 else over_down
        scaled[n] = (held[n].astype(F32) * over).astype(BF)
        stores[n].start()
    for store in stores:
        store.wait()


def shards(tokens, gate_weight, up_weight, down_weight, out_grad, amax_prior):
    vmem = pl.BlockSpec(memory_space=pltpu.VMEM)
    hbm = pl.BlockSpec(memory_space=pl.ANY)
    V = pltpu.VMEM
    sum_scratch = (
        V((4, 2, 4, 16, 2048), BF), V((4, 2, 4, 16, HALF), BF),
        V((3, 2, 4, 16, 512), BF), V((3, 4, 2, 16, 512), BF),
        V((2, 4, 16, 512), BF), V((4, 2, 16, 512), BF),
        V((3, 2, 16, 512), BF), V((3, 2, 16, 512), BF),
        V((2, 16, HALF), F32), V((16, HALF), F32), V((16, HALF), F32), V((8, HALF), F32),
    )
    output, input_grad, wide, wdown, peaks = pl.pallas_call(
        kernel,
        out_shape=(
            jax.ShapeDtypeStruct((8, 2048), BF),
            jax.ShapeDtypeStruct((8, 2048), BF),
            jax.ShapeDtypeStruct((WIDE, 2048), BF),
            jax.ShapeDtypeStruct((UNITS, 2048), BF),
            jax.ShapeDtypeStruct((16, 128), F32),
        ),
        in_specs=[pl.BlockSpec(memory_space=pltpu.SMEM), vmem, vmem, hbm, hbm, hbm],
        out_specs=(vmem, vmem, hbm, hbm, vmem),
        scratch_shapes=[
            V((4, 2, 4, 16, 2048), BF), V((4, 2, 4, 16, 2048), BF),
            V((WIDE, 2048), BF), V((UNITS, 2048), BF),
            V((16, 2048), F32), V((16, HALF), F32),
            V((2, WIDE, 128), BF), V((2, WIDE, 128), F32), V((2, WIDE, 128), BF),
            V((WIDE, 128), BF), V((WIDE, 128), BF),
            V((2, UNITS, 128), BF), V((2, UNITS, 128), F32), V((2, UNITS, 128), BF),
            V((UNITS, 128), BF), V((UNITS, 128), BF),
            V((4, UNITS, 128), BF), V((4, WIDE, 128), BF),
            sum_scratch, sum_scratch,
            V((WIDE, 2048), BF), V((UNITS, 2048), BF),
            V((3, 8, 128), F32), V((3, 7, 8, 128), F32),
            pltpu.SemaphoreType.DMA((N_SEMS,)), pltpu.SemaphoreType.DMA((N_SEMS,)),
            pltpu.SemaphoreType.DMA((3,)), pltpu.SemaphoreType.DMA((2,)),
        ],
        compiler_params=pltpu.CompilerParams(
            collective_id=0, has_side_effects=True, vmem_limit_bytes=60 << 20
        ),
        name="layer",
    )(amax_prior, tokens, out_grad, gate_weight.T, up_weight.T, down_weight)
    full = (
        jax.ShapeDtypeStruct((UNITS, 2048), BF),
        jax.ShapeDtypeStruct((UNITS, 2048), BF),
        jax.ShapeDtypeStruct((UNITS, 2048), BF),
        jax.ShapeDtypeStruct((8, 2048), BF),
        jax.ShapeDtypeStruct((8, 2048), BF),
        jax.ShapeDtypeStruct((6,), F32),
    )
    smem = pl.BlockSpec(memory_space=pltpu.SMEM)
    gate_grad, up_grad, down_grad, output, input_grad, amaxes = pl.pallas_call(
        scale_grads,
        out_shape=full,
        in_specs=[smem, vmem, vmem, hbm, hbm],
        out_specs=(hbm, hbm, hbm, vmem, vmem, smem),
        scratch_shapes=[
            V((6, UNITS // 2, 2048), BF),
            V((6, UNITS // 2, 2048), BF),
            pltpu.SemaphoreType.DMA((6,)),
            pltpu.SemaphoreType.DMA((6,)),
        ],
        compiler_params=pltpu.CompilerParams(vmem_limit_bytes=60 << 20),
        name="scale",
    )(peaks, output, input_grad, wide, wdown)
    return (output, input_grad, gate_grad.T, up_grad.T, down_grad, amaxes)


def solution(mesh):
    placed = (
        P("hid", "tok"),
        P("tok", "hid"),
        P("tok", "hid"),
        P("hid", "tok"),
        P("hid", "tok"),
        P(),
    )
    return jax.shard_map(
        shards,
        mesh=mesh,
        in_specs=placed,
        out_specs=(
            P("hid", "tok"),
            P("hid", "tok"),
            P("tok", "hid"),
            P("tok", "hid"),
            P("hid", "tok"),
            P(),
        ),
        check_vma=False,
    )
```

time: 157 us -> 118 us (0.75)
  local copies, waits for them, and re-layouts: 16.5 us -> 0 us
  other arithmetic: 12.8 us -> 0 us
  Pallas kernels: 125 us -> 117 us
    unnamed x10 -> x0, local copies, waits for them, and re-layouts: 13.9 us -> none
    pallas_call x1, Pallas kernels: 125 us -> 112 us  [shards(): pl.pallas_call(kernel, out_shape=(jax.ShapeDtypeStruct((8, 2048), BF), ja...]
    convert_element_type x2 -> x0, other arithmetic: 7.77 us -> none  [the longest x1 4.72 us: shards(): up_grad = (wide[:, width:2 * width].astype(F32) / wide_top).astype(BF)]
    pallas_call x0 -> x1, Pallas kernels: none -> 5.56 us  [shards(): pl.pallas_call(scale_grads, out_shape=full, in_specs=[smem, vmem, vmem, h...]
    concatenate x1 -> x0, other arithmetic: 5.04 us -> none  [shards(): jnp.concatenate([gate_weight, up_weight, jnp.zeros((2048, WIDE - 2 * widt...]
    slice x2 -> x0, local copies, waits for them, and re-layouts: 2.58 us -> none  [the longest x1 1.31 us: shards(): return (output, input_grad, gate_grad, up_grad, down_grad, peaks[8:14, 0])]
where the time goes in v2:
time: 118 us
  Pallas kernels  117 us (99%)
    pallas_call x1, Pallas kernels, shards(): pl.pallas_call(kernel, out_shape=(jax.ShapeDtypeStruct((8, 2048), BF), ja...  112 us
    pallas_call x1, Pallas kernels, shards(): pl.pallas_call(scale_grads, out_shape=full, in_specs=[smem, vmem, vmem, h...  5.56 us

profile of v2, /device:TPU:1, one launch (start us, length us, event | category | flops | bytes accessed | tf_op | source)
XLA Modules:
  0.0 118.0 jit_solution(16077364758670348966)
XLA Ops:
  0.6 111.6 %layer.1 = (bf16[8,2048]{1,0:T(8,128)(2,1)}, bf16[8,2048]{1,0:T(8,128)(2,1)}, bf16[832,2048]{1,0:T(8,128)(2,1)}, bf16[416,2048]{1,0:T(8,128)(2,1)}, f32[16,128]{1,0:T(8,128)}) custom-call(f32[4]{0:T(128)} %prior.1, bf16[8,2048]{1,0:T(8,128)(2,1)} %tokens.1, bf16[8,2048]{1,0:T(8,128)(2,1)} %out_grad.1, bf16[416,2048]{1,0:T(8,128)(2,1)} %bitcast.4, ...), custom_call_target="tpu_custom_call" | custom-call | tf_op jit(solution)/shard_map/layer/pallas_call | solution.py:528
  112.3 5.6 %scale.1 = (bf16[416,2048]{1,0:T(8,128)(2,1)}, bf16[416,2048]{1,0:T(8,128)(2,1)}, bf16[416,2048]{1,0:T(8,128)(2,1)}, bf16[8,2048]{1,0:T(8,128)(2,1)}, bf16[8,2048]{1,0:T(8,128)(2,1)}, /*index=5*/f32[6]{0:T(128)}) custom-call(f32[16,128]{1,0:T(8,128)} %get-tuple-element.17.peaks, bf16[8,2048]{1,0:T(8,128)(2,1)} %get-tuple-element.18.out_in, ...), custom_call_target="tpu_custom_call" | custom-call | tf_op jit(solution)/shard_map/scale/pallas_call | solution.py:568

commit v3 on v2

--- a/solution.py
+++ b/solution.py
@@ -57,7 +57,7 @@
             copy.wait_send()
 
 
-N_SEMS = 240
+N_SEMS = 260
 
 
 def kernel(
@@ -86,6 +86,7 @@
     peers = [device(dx=d, dc=e) for d in range(4) for e in range(2) if d or e]
     peers += [device(dy=d) for d in (1, 2, 3)]
     peers += [device(dt=d, dz=e) for d in range(4) for e in range(2) if d or e]
+    peers += [device(dz=1, dc=1)]
     barrier = pltpu.get_barrier_semaphore()
     for peer in peers:
         pl.semaphore_signal(barrier, inc=1, device_id=peer, device_id_type=MESH)
@@ -106,51 +107,49 @@
     og_f = out_grad[...].astype(F32)
     max_x = jnp.max(jnp.abs(tok_f))
     max_g = jnp.max(jnp.abs(og_f))
-    swap_out[pl.ds(0, 8), :] = quantize(tok_f, s0).astype(F32)
-    swap_out[pl.ds(8, 8), :] = quantize(og_f, s2).astype(F32)
+    swap_out[...] = jnp.concatenate(
+        [quantize(tok_f, s0).astype(F32), quantize(og_f, s2).astype(F32)], axis=0
+    ).astype(BF)
 
     links = Links(send_sem, recv_sem)
     core = device(dc=1)
 
     pl.semaphore_wait(barrier, len(peers))
 
-    slot = links.slots(1)
-    links.start(swap_out.at[:, other], swap_in, slot, core)
-    links.arrived(swap_in, slot, core)
-    own = swap_out[:, mine]
-    theirs = swap_in[...]
-    low = jnp.where(c == 0, own, theirs)
-    high = jnp.where(c == 0, theirs, own)
-    xb[y, zh, x, :, mine] = jnp.concatenate([low[0:8], high[0:8]], axis=0).astype(BF)
-    gb[y, zh, x, :, mine] = jnp.concatenate([low[8:16], high[8:16]], axis=0).astype(BF)
-
+    first = links.slots(3)
+    away = device(dz=1)
+    across = device(dz=1, dc=1)
+    links.start(swap_out.at[:, mine], swap_in.at[1], first + 1, away)
+    links.start(swap_out.at[:, other], swap_in.at[2], first + 2, across)
+    links.start(swap_out.at[:, other], swap_in.at[0], first, core)
+
+    def place(z, own, theirs):
+        own, theirs = own.astype(F32), theirs.astype(F32)
+        low = jnp.where(c == 0, own, theirs)
+        high = jnp.where(c == 0, theirs, own)
+        xb[y, z, x, :, mine] = jnp.concatenate([low[0:8], high[0:8]], axis=0).astype(BF)
+        gb[y, z, x, :, mine] = jnp.concatenate([low[8:16], high[8:16]], axis=0).astype(BF)
+
+    links.arrived(swap_in.at[0], first, core)
+    place(zh, swap_out[:, mine], swap_in[0])
     def step_x(d):
         return device(dx=d)
 
     def step_y(d):
         return device(dy=d)
 
-    away = device(dz=1)
     cols_xy = pl.ds(pl.multiple_of(c * HALF, 512), 512)
     cols_yx = pl.ds(pl.multiple_of(c * HALF + 512, 512), 512)
 
     class Gather:
         def __init__(self, buf):
             self.buf = buf
-            self.z = links.slots(1)
             self.first = {a: (links.slots(4), links.slots(4)) for a in (0, 1)}
             self.second = {a: (links.slots(4), links.slots(4)) for a in (0, 1)}
-            self.swap = (links.slots(4), links.slots(4))
+            self.swap = {a: (links.slots(4), links.slots(4)) for a in (0, 1)}
 
         def level(self, a):
             return zh if a == 0 else 1 - zh
-
-        def send_z(self):
-            block = self.buf.at[y, zh, x, :, mine]
-            links.start(block, block, self.z, away)
-
-        def wait_z(self):
-            links.arrived(self.buf.at[y, 1 - zh, x, :, mine], self.z, away)
 
         def send_first(self, a):
             z = self.level(a)
@@ -176,50 +175,59 @@
                 rows = self.buf.at[:, z, x, :, cols_yx]
                 links.start(rows, rows, self.second[a][1] + d, step_x(d))
 
-        def wait_second(self, d):
-            for a in (0, 1):
-                z = self.level(a)
-                rows = self.buf.at[(y - d) % 4, z, :, :, cols_xy]
-                links.arrived(rows, self.second[a][0] + d, step_y(4 - d))
-                rows = self.buf.at[:, z, (x - d) % 4, :, cols_yx]
-                links.arrived(rows, self.second[a][1] + d, step_x(4 - d))
-
-        def send_swap(self, d):
-            rows = self.buf.at[(y - d) % 4, :, :, :, cols_xy]
-            links.start(rows, rows, self.swap[0] + d, core)
-            rows = self.buf.at[:, :, (x - d) % 4, :, cols_yx]
-            links.start(rows, rows, self.swap[1] + d, core)
-
-        def wait_swap(self):
+        def wait_second(self, a, d):
+            z = self.level(a)
+            rows = self.buf.at[(y - d) % 4, z, :, :, cols_xy]
+            links.arrived(rows, self.second[a][0] + d, step_y(4 - d))
+            rows = self.buf.at[:, z, (x - d) % 4, :, cols_yx]
+            links.arrived(rows, self.second[a][1] + d, step_x(4 - d))
+
+        def send_swap(self, a, d):
+            z = self.level(a)
+            rows = self.buf.at[(y - d) % 4, z, :, :, cols_xy]
+            links.start(rows, rows, self.swap[a][0] + d, core)
+            rows = self.buf.at[:, z, (x - d) % 4, :, cols_yx]
+            links.start(rows, rows, self.swap[a][1] + d, core)
+
+        def wait_swap(self, a):
+            z = self.level(a)
             there_xy = pl.ds(pl.multiple_of((1 - c) * HALF, 512), 512)
             there_yx = pl.ds(pl.multiple_of((1 - c) * HALF + 512, 512), 512)
             for d in (0, 1, 3, 2):
-                rows = self.buf.at[(y - d) % 4, :, :, :, there_xy]
-                links.arrived(rows, self.swap[0] + d, core)
-                rows = self.buf.at[:, :, (x - d) % 4, :, there_yx]
-                links.arrived(rows, self.swap[1] + d, core)
+                rows = self.buf.at[(y - d) % 4, z, :, :, there_xy]
+                links.arrived(rows, self.swap[a][0] + d, core)
+                rows = self.buf.at[:, z, (x - d) % 4, :, there_yx]
+                links.arrived(rows, self.swap[a][1] + d, core)
+
+        def complete(self, a):
+            for d in (1, 3, 2):
+                self.wait_second(a, d)
+                self.send_swap(a, d)
+            self.wait_swap(a)
 
     gx, gg = Gather(xb), Gather(gb)
-    gx.send_z()
     gx.send_first(0)
-    gg.send_z()
     gg.send_first(0)
-    gx.wait_z()
+    gx.wait_first(0)
+    gx.send_second(0)
+    links.arrived(swap_in.at[1], first + 1, away)
+    links.arrived(swap_in.at[2], first + 2, across)
+    place(1 - zh, swap_in[1], swap_in[2])
     gx.send_first(1)
-    gg.wait_z()
     gg.send_first(1)
-    for gather in (gx, gg):
-        gather.wait_first(0)
-        gather.send_second(0)
-        gather.wait_first(1)
-        gather.send_second(1)
-        gather.send_swap(0)
+    gx.send_swap(0, 0)
+    gg.wait_first(0)
+    gg.send_second(0)
+    gx.wait_first(1)
+    gx.send_second(1)
+    gg.wait_first(1)
+    gg.send_second(1)
+    gx.send_swap(1, 0)
+    gg.send_swap(0, 0)
+    gg.send_swap(1, 0)
     for load in loads:
         load.wait()
-    for d in (1, 3, 2):
-        gx.wait_second(d)
-        gx.send_swap(d)
-    gx.wait_swap()
+    gx.complete(0)
 
     order = ((1 - p) + 2 * (1 - s), (1 - p) + 2 * s, p + 2 * (1 - s), p + 2 * s)
     r1, r2 = links.slots(4), links.slots(2)
@@ -227,23 +235,37 @@
     partner = beside()
     far = device(dt=2)
     units = (pl.ds(0, UNITS), pl.ds(UNITS, UNITS))
-
-    def pair(buf, j):
-        two = [buf[(y + k) % 4].reshape(128, 2048) for k in order[j : j + 2]]
-        return jnp.concatenate(two, axis=0)
-
-    value = contract_last(wide_w[...], pair(xb, 0))
-    for j, to in ((0, 1 - s), (1, s)):
-        part[j] = value[:, 128 * j : 128 * j + 128].astype(BF)
-        for u in (0, 1):
-            links.start(part.at[j, units[u]], got1.at[to, units[u]], r1 + 2 * to + u, partner)
-    value = contract_last(wide_w[...], pair(xb, 2))
-    keep[0] = value[:, :128]
-    keep[1] = value[:, 128:]
-    for d in (1, 3, 2):
-        gg.wait_second(d)
-        gg.send_swap(d)
-    gg.wait_swap()
+    lower = lax.broadcasted_iota(jnp.int32, (UNITS, 128), 1) < 64
+
+    def turn(value):
+        return pltpu.roll(value, 64, 1)
+
+    def pair(buf, j, z=None):
+        two = [buf[(y + k) % 4] if z is None else buf[(y + k) % 4, z] for k in order[j : j + 2]]
+        return jnp.concatenate([value.reshape(-1, 2048) for value in two], axis=0)
+
+    def gate_and_up(j, z):
+        value = contract_last(wide_w[...], pair(xb, j, z))
+        gate, up = value[:UNITS], value[UNITS:]
+        return jnp.where(lower, gate, turn(up)), jnp.where(lower, turn(gate), up)
+
+    for a, z in ((0, zh), (1, 1 - zh)):
+        if a:
+            gx.complete(1)
+        for j, to, value in zip((0, 1), (1 - s, s), gate_and_up(0, z)):
+            part[j, a] = value.astype(BF)
+            links.start(part.at[j, a], got1.at[to, z], r1 + 2 * to + a, partner)
+        for j, value in zip((0, 1), gate_and_up(2, z)):
+            keep[j, z] = value
+
+    def send_far(a, z):
+        links.arrived(got1.at[1 - s, z], r1 + 2 * (1 - s) + a, partner)
+        send2[z] = (keep[0, z] + got1[1 - s, z].astype(F32)).astype(BF)
+        links.start(send2.at[z], got2.at[z], r2 + a, far)
+
+    send_far(0, zh)
+    gg.complete(0)
+    gg.complete(1)
     value = contract_last(down_w[...], pair(gb, 0))
     for j, to in ((0, 1 - s), (1, s)):
         dpart[j] = value[:, 128 * j : 128 * j + 128].astype(BF)
@@ -251,10 +273,7 @@
     value = contract_last(down_w[...], pair(gb, 2))
     dkeep[0] = value[:, :128]
     dkeep[1] = value[:, 128:]
-    for u in (0, 1):
-        links.arrived(got1.at[1 - s, units[u]], r1 + 2 * (1 - s) + u, partner)
-        send2[units[u], :] = (keep[0, units[u]] + got1[1 - s, units[u]].astype(F32)).astype(BF)
-        links.start(send2.at[units[u]], got2.at[units[u]], r2 + u, far)
+    send_far(1, 1 - zh)
     links.arrived(dgot1.at[1 - s], d1 + (1 - s), partner)
     dsend2[...] = (dkeep[0] + dgot1[1 - s].astype(F32)).astype(BF)
     links.start(dsend2, dgot2, d2, far)
@@ -262,12 +281,14 @@
     h1, h2, h3 = links.slots(1), links.slots(1), links.slots(1)
     g1, g2, g3 = links.slots(2), links.slots(2), links.slots(2)
 
-    for u in (0, 1):
-        links.arrived(got1.at[s, units[u]], r1 + 2 * s + u, partner)
-        links.arrived(got2.at[units[u]], r2 + u, far)
-    both = (keep[1] + got1[s].astype(F32) + got2[...].astype(F32)) * s0
-    gate = both[:UNITS]
-    up = both[UNITS:]
+    for a, z in ((0, zh), (1, 1 - zh)):
+        links.arrived(got1.at[s, z], r1 + 2 * s + a, partner)
+        links.arrived(got2.at[z], r2 + a, far)
+    low, high = [
+        (keep[1, z] + got1[s, z].astype(F32) + got2[z].astype(F32)) * s0 for z in (0, 1)
+    ]
+    gate = jnp.where(lower, low, turn(high))
+    up = jnp.where(lower, turn(low), high)
     sig = jax.nn.sigmoid(gate)
     act = gate * sig
     hidden = act * up
@@ -294,12 +315,12 @@
     links.start(hb.at[yf], hb.at[yf], h3, partner)
 
     class Spread:
-        def __init__(self, part, core_in, ring_y, ring_x, then_x, then_y, got_x, got_y, zs, zr, fin, fr):
+        def __init__(self, part, core_in, ring_y, ring_x, then_x, then_y, got_x, got_y, zs, fr):
             self.part, self.core_in, self.ring_y, self.ring_x = part, core_in, ring_y, ring_x
             self.then_x, self.then_y, self.got_x, self.got_y = then_x, then_y, got_x, got_y
-            self.zs, self.zr, self.fin, self.fr = zs, zr, fin, fr
+            self.zs, self.fr = zs, fr
             self.cores, self.yx, self.xy = links.slots(4), links.slots(4), links.slots(16)
-            self.x, self.y, self.z, self.c = links.slots(4), links.slots(4), links.slots(1), links.slots(1)
+            self.x, self.y, self.z = links.slots(4), links.slots(4), links.slots(3)
 
         def block(self, n, left, right):
             value = contract_first(left, right)
@@ -354,17 +375,16 @@
             for d in (1, 2, 3):
                 total = total + self.got_y[d - 1].astype(F32)
             self.zs[:, :, right] = total
-            links.start(self.zs.at[1 - zh], self.zr, self.z, away)
-
-        def fourth(self):
-            links.arrived(self.zr, self.z, away)
-            self.fin[...] = self.zs[zh] + self.zr[...]
-            links.start(self.fin.at[rows_other], self.fr, self.c, core)
+            links.start(self.zs.at[1 - zh, rows_mine], self.fr.at[1], self.z + 1, away)
+            links.start(self.zs.at[1 - zh, rows_other], self.fr.at[2], self.z + 2, across)
+            links.start(self.zs.at[zh, rows_other], self.fr.at[0], self.z, core)
 
         def last(self, ref, scale):
-            links.arrived(self.fr, self.c, core)
-            ref[:, mine] = (self.fin[rows_mine, :] * scale).astype(BF)
-            ref[:, other] = (self.fr[...] * scale).astype(BF)
+            links.arrived(self.fr.at[0], self.z, core)
+            links.arrived(self.fr.at[1], self.z + 1, away)
+            links.arrived(self.fr.at[2], self.z + 2, across)
+            ref[:, mine] = ((self.zs[zh, rows_mine, :] + self.fr[1]) * scale).astype(BF)
+            ref[:, other] = ((self.fr[0] + self.fr[2]) * scale).astype(BF)
 
         def finish(self):
             for d in (1, 2, 3):
@@ -430,9 +450,9 @@
         return jnp.maximum(top, jnp.max(jnp.abs(value)))
 
     in_sum.first(2)
-    max_w = lax.fori_loop(0, 2, wide_tile, jnp.float32(0.0))
+    max_w = lax.fori_loop(0, 3, wide_tile, jnp.float32(0.0))
     in_sum.first(3)
-    max_w = lax.fori_loop(2, 8, wide_tile, max_w)
+    max_w = lax.fori_loop(3, 8, wide_tile, max_w)
     store_w = pltpu.make_async_copy(wide_g, wide_hbm, store_sem.at[1])
     store_w.start()
 
@@ -462,12 +482,10 @@
     in_sum.second()
     tops = take_tops(0, tops, plane, first)
     first = send_tops(1, tops, column)
-    out_sum.fourth()
     in_sum.third()
     tops = take_tops(1, tops, column, first)
     first = send_tops(2, tops, depth)
     out_sum.last(out_ref, s1)
-    in_sum.fourth()
     tops = take_tops(2, tops, depth, first)
     peaks_ref[pl.ds(0, 8), :] = tops
     peaks_ref[pl.ds(8, 8), :] = jnp.log(tops + 1e-6)
@@ -523,7 +541,7 @@
         V((3, 2, 4, 16, 512), BF), V((3, 4, 2, 16, 512), BF),
         V((2, 4, 16, 512), BF), V((4, 2, 16, 512), BF),
         V((3, 2, 16, 512), BF), V((3, 2, 16, 512), BF),
-        V((2, 16, HALF), F32), V((16, HALF), F32), V((16, HALF), F32), V((8, HALF), F32),
+        V((2, 16, HALF), F32), V((3, 8, HALF), F32),
     )
     output, input_grad, wide, wdown, peaks = pl.pallas_call(
         kernel,
@@ -539,9 +557,9 @@
         scratch_shapes=[
             V((4, 2, 4, 16, 2048), BF), V((4, 2, 4, 16, 2048), BF),
             V((WIDE, 2048), BF), V((UNITS, 2048), BF),
-            V((16, 2048), F32), V((16, HALF), F32),
-            V((2, WIDE, 128), BF), V((2, WIDE, 128), F32), V((2, WIDE, 128), BF),
-            V((WIDE, 128), BF), V((WIDE, 128), BF),
+            V((16, 2048), BF), V((3, 16, HALF), BF),
+            V((2, 2, UNITS, 128), BF), V((2, 2, UNITS, 128), F32), V((2, 2, UNITS, 128), BF),
+            V((2, UNITS, 128), BF), V((2, UNITS, 128), BF),
             V((2, UNITS, 128), BF), V((2, UNITS, 128), F32), V((2, UNITS, 128), BF),
             V((UNITS, 128), BF), V((UNITS, 128), BF),
             V((4, UNITS, 128), BF), V((4, WIDE, 128), BF),

time: 118 us -> 109 us (0.924)
  Pallas kernels: 117 us -> 108 us
    pallas_call x1, Pallas kernels: 112 us -> 102 us  [shards(): pl.pallas_call(kernel, out_shape=(jax.ShapeDtypeStruct((8, 2048), BF), ja...]
where the time goes in v3:
time: 109 us; the launch traced here: 108 us
  Pallas kernels  108 us (99%)
    pallas_call x1, Pallas kernels, shards(): pl.pallas_call(kernel, out_shape=(jax.ShapeDtypeStruct((8, 2048), BF), ja...  102 us
    pallas_call x1, Pallas kernels, shards(): pl.pallas_call(scale_grads, out_shape=full, in_specs=[smem, vmem, vmem, h...  5.56 us

profile of v3, /device:TPU:1, one launch (start us, length us, event | category | flops | bytes accessed | tf_op | source)
XLA Modules:
  0.0 108.4 jit_solution(11711692036535242685)
XLA Ops:
  0.6 102.0 %layer.1 = (bf16[8,2048]{1,0:T(8,128)(2,1)}, bf16[8,2048]{1,0:T(8,128)(2,1)}, bf16[832,2048]{1,0:T(8,128)(2,1)}, bf16[416,2048]{1,0:T(8,128)(2,1)}, f32[16,128]{1,0:T(8,128)}) custom-call(f32[4]{0:T(128)} %prior.1, bf16[8,2048]{1,0:T(8,128)(2,1)} %tokens.1, bf16[8,2048]{1,0:T(8,128)(2,1)} %out_grad.1, bf16[416,2048]{1,0:T(8,128)(2,1)} %bitcast.4, ...), custom_call_target="tpu_custom_call" | custom-call | tf_op jit(solution)/shard_map/layer/pallas_call | solution.py:546
  102.7 5.6 %scale.1 = (bf16[416,2048]{1,0:T(8,128)(2,1)}, bf16[416,2048]{1,0:T(8,128)(2,1)}, bf16[416,2048]{1,0:T(8,128)(2,1)}, bf16[8,2048]{1,0:T(8,128)(2,1)}, bf16[8,2048]{1,0:T(8,128)(2,1)}, /*index=5*/f32[6]{0:T(128)}) custom-call(f32[16,128]{1,0:T(8,128)} %get-tuple-element.17.peaks, bf16[8,2048]{1,0:T(8,128)(2,1)} %get-tuple-element.18.out_in, ...), custom_call_target="tpu_custom_call" | custom-call | tf_op jit(solution)/shard_map/scale/pallas_call | solution.py:586

commit v4 on v3

--- a/solution.py
+++ b/solution.py
@@ -267,9 +267,9 @@
     gg.complete(0)
     gg.complete(1)
     value = contract_last(down_w[...], pair(gb, 0))
-    for j, to in ((0, 1 - s), (1, s)):
-        dpart[j] = value[:, 128 * j : 128 * j + 128].astype(BF)
-        links.start(dpart.at[j], dgot1.at[to], d1 + to, partner)
+    dpart[0] = value[:, :128].astype(BF)
+    dpart[1] = value[:, 128:].astype(BF)
+    links.start(dpart.at[0], dgot1.at[1 - s], d1 + (1 - s), partner)
     value = contract_last(down_w[...], pair(gb, 2))
     dkeep[0] = value[:, :128]
     dkeep[1] = value[:, 128:]
@@ -277,6 +277,7 @@
     links.arrived(dgot1.at[1 - s], d1 + (1 - s), partner)
     dsend2[...] = (dkeep[0] + dgot1[1 - s].astype(F32)).astype(BF)
     links.start(dsend2, dgot2, d2, far)
+    links.start(dpart.at[1], dgot1.at[s], d1 + s, partner)
     yt = (y + t) % 4
     h1, h2, h3 = links.slots(1), links.slots(1), links.slots(1)
     g1, g2, g3 = links.slots(2), links.slots(2), links.slots(2)
@@ -399,19 +400,24 @@
     out_sum = Spread(*o_refs)
     in_sum = Spread(*i_refs)
 
-    for n in (0, 1):
-        out_sum.block(n, hb[blocks[n]], down_w[...])
-    links.arrived(hb.at[yp], h2, partner)
-    out_sum.block(2, hb[yp], down_w[...])
-    links.arrived(hb.at[ypf], h3, partner)
-    out_sum.block(3, hb[ypf], down_w[...])
-    for n in range(4):
-        out_sum.first(n)
-
     def pass_on():
         for u in (0, 1):
             links.arrived(db.at[yf, units[u]], g1 + u, far)
             links.start(db.at[yf, units[u]], db.at[yf, units[u]], g3 + u, partner)
+
+    out_sum.block(0, hb[yt], down_w[...])
+    out_sum.block(1, hb[yf], down_w[...])
+    links.arrived(hb.at[yp], h2, partner)
+    out_sum.block(2, hb[yp], down_w[...])
+    in_sum.block(0, db[yt], wide_w[...])
+    for n in range(3):
+        out_sum.first(n)
+    in_sum.first(0)
+    pass_on()
+    in_sum.block(1, db[yf], wide_w[...])
+    links.arrived(hb.at[ypf], h3, partner)
+    out_sum.block(3, hb[ypf], down_w[...])
+    in_sum.first(1)
 
     hq_all = jnp.concatenate([hb[n] for n in range(4)], axis=1)
 
@@ -423,19 +429,14 @@
         return jnp.maximum(top, jnp.max(jnp.abs(value)))
 
     max_d = lax.fori_loop(0, 4, down_tile, jnp.float32(0.0))
-    pass_on()
-    in_sum.block(0, db[yt], wide_w[...])
-    in_sum.block(1, db[yf], wide_w[...])
-    out_sum.second()
+    out_sum.first(3)
+    for u in (0, 1):
+        links.arrived(db.at[yp, units[u]], g2 + u, partner)
+    in_sum.block(2, db[yp], wide_w[...])
     max_d = lax.fori_loop(4, 8, down_tile, max_d)
     store_d = pltpu.make_async_copy(down_g, wdown_hbm, store_sem.at[0])
     store_d.start()
-    in_sum.first(0)
-    in_sum.first(1)
-    for u in (0, 1):
-        links.arrived(db.at[yp, units[u]], g2 + u, partner)
-    in_sum.block(2, db[yp], wide_w[...])
-    out_sum.third()
+    in_sum.first(2)
     for u in (0, 1):
         links.arrived(db.at[ypf, units[u]], g3 + u, partner)
     in_sum.block(3, db[ypf], wide_w[...])
@@ -449,10 +450,9 @@
         wide_g[:, columns] = value.astype(BF)
         return jnp.maximum(top, jnp.max(jnp.abs(value)))
 
-    in_sum.first(2)
-    max_w = lax.fori_loop(0, 3, wide_tile, jnp.float32(0.0))
+    max_w = lax.fori_loop(0, 4, wide_tile, jnp.float32(0.0))
     in_sum.first(3)
-    max_w = lax.fori_loop(3, 8, wide_tile, max_w)
+    max_w = lax.fori_loop(4, 8, wide_tile, max_w)
     store_w = pltpu.make_async_copy(wide_g, wide_hbm, store_sem.at[1])
     store_w.start()
 
@@ -479,9 +479,11 @@
     depth = [dict(dt=d, dz=e) for d in range(4) for e in range(2) if d or e]
     column = [dict(dy=d) for d in (1, 2, 3)]
     first = send_tops(0, tops, plane)
+    out_sum.second()
     in_sum.second()
     tops = take_tops(0, tops, plane, first)
     first = send_tops(1, tops, column)
+    out_sum.third()
     in_sum.third()
     tops = take_tops(1, tops, column, first)
     first = send_tops(2, tops, depth)
@@ -504,10 +506,8 @@
     gate_out, up_out, down_out, out_ref, in_grad_ref, amaxes_ref,
     held, scaled, load_sem, store_sem,
 ):
-    size = UNITS // 2
-    halves = [pl.ds(n * size, size) for n in range(4)]
-    sources = [wide_hbm.at[rows] for rows in halves] + [wdown_hbm.at[rows] for rows in halves[:2]]
-    targets = [ref.at[rows] for ref in (gate_out, up_out, down_out) for rows in halves[:2]]
+    sources = [wide_hbm.at[pl.ds(0, UNITS)], wide_hbm.at[pl.ds(UNITS, UNITS)], wdown_hbm]
+    targets = [gate_out, up_out, down_out]
     loads = [
         pltpu.make_async_copy(source, held.at[n], load_sem.at[n]) for n, source in enumerate(sources)
     ]
@@ -523,9 +523,9 @@
     in_grad_ref[...] = in_grad_in[...]
     over_wide = 1.0 / (peaks[4, 0] + 1e-6)
     over_down = 1.0 / (peaks[5, 0] + 1e-6)
-    for n in range(6):
+    for n in range(3):
         loads[n].wait()
-        over = over_wide if n < 4 else over_down
+        over = over_wide if n < 2 else over_down
         scaled[n] = (held[n].astype(F32) * over).astype(BF)
         stores[n].start()
     for store in stores:
@@ -589,10 +589,10 @@
         in_specs=[smem, vmem, vmem, hbm, hbm],
         out_specs=(hbm, hbm, hbm, vmem, vmem, smem),
         scratch_shapes=[
-            V((6, UNITS // 2, 2048), BF),
-            V((6, UNITS // 2, 2048), BF),
-            pltpu.SemaphoreType.DMA((6,)),
-            pltpu.SemaphoreType.DMA((6,)),
+            V((3, UNITS, 2048), BF),
+            V((3, UNITS, 2048), BF),
+            pltpu.SemaphoreType.DMA((3,)),
+            pltpu.SemaphoreType.DMA((3,)),
         ],
         compiler_params=pltpu.CompilerParams(vmem_limit_bytes=60 << 20),
         name="scale",

time: 109 us -> 103 us (0.945)
  Pallas kernels: 108 us -> 101 us
    pallas_call x1, Pallas kernels: 102 us -> 96 us  [shards(): pl.pallas_call(kernel, out_shape=(jax.ShapeDtypeStruct((8, 2048), BF), ja...]
where the time goes in v4:
time: 103 us; the launch traced here: 102 us
  Pallas kernels  101 us (98%)
    pallas_call x1, Pallas kernels, shards(): pl.pallas_call(kernel, out_shape=(jax.ShapeDtypeStruct((8, 2048), BF), ja...  96 us
    pallas_call x1, Pallas kernels, shards(): pl.pallas_call(scale_grads, out_shape=full, in_specs=[smem, vmem, vmem, h...  5.52 us

profile of v4, /device:TPU:1, one launch (start us, length us, event | category | flops | bytes accessed | tf_op | source)
XLA Modules:
  0.0 102.3 jit_solution(6691128007563840007)
XLA Ops:
  0.6 96.0 %layer.1 = (bf16[8,2048]{1,0:T(8,128)(2,1)}, bf16[8,2048]{1,0:T(8,128)(2,1)}, bf16[832,2048]{1,0:T(8,128)(2,1)}, bf16[416,2048]{1,0:T(8,128)(2,1)}, f32[16,128]{1,0:T(8,128)}) custom-call(f32[4]{0:T(128)} %prior.1, bf16[8,2048]{1,0:T(8,128)(2,1)} %tokens.1, bf16[8,2048]{1,0:T(8,128)(2,1)} %out_grad.1, bf16[416,2048]{1,0:T(8,128)(2,1)} %bitcast.4, ...), custom_call_target="tpu_custom_call" | custom-call | tf_op jit(solution)/shard_map/layer/pallas_call | solution.py:546
  96.6 5.5 %scale.1 = (bf16[416,2048]{1,0:T(8,128)(2,1)}, bf16[416,2048]{1,0:T(8,128)(2,1)}, bf16[416,2048]{1,0:T(8,128)(2,1)}, bf16[8,2048]{1,0:T(8,128)(2,1)}, bf16[8,2048]{1,0:T(8,128)(2,1)}, /*index=5*/f32[6]{0:T(128)}) custom-call(f32[16,128]{1,0:T(8,128)} %get-tuple-element.17.peaks, bf16[8,2048]{1,0:T(8,128)(2,1)} %get-tuple-element.18.out_in, ...), custom_call_target="tpu_custom_call" | custom-call | tf_op jit(solution)/shard_map/scale/pallas_call | solution.py:586

commit v5 on v4

--- a/solution.py
+++ b/solution.py
@@ -23,6 +23,15 @@
 
 def quantize(value, scale):
     return jnp.clip(value / scale, -448.0, 448.0).astype(BF)
+
+
+def fold(value):
+    return jnp.concatenate([value[:, :512], value[:, 512:]], axis=0).astype(BF)
+
+
+def unfold(value):
+    value = value.astype(F32)
+    return jnp.concatenate([value[:8], value[8:]], axis=1)
 
 
 class Links:
@@ -107,31 +116,39 @@
     og_f = out_grad[...].astype(F32)
     max_x = jnp.max(jnp.abs(tok_f))
     max_g = jnp.max(jnp.abs(og_f))
-    swap_out[...] = jnp.concatenate(
-        [quantize(tok_f, s0).astype(F32), quantize(og_f, s2).astype(F32)], axis=0
-    ).astype(BF)
+    for n, value in enumerate((quantize(tok_f, s0), quantize(og_f, s2))):
+        value = value.astype(F32)
+        swap_out[n, 0] = fold(value[:, :HALF])
+        swap_out[n, 1] = fold(value[:, HALF:])
 
     links = Links(send_sem, recv_sem)
     core = device(dc=1)
 
     pl.semaphore_wait(barrier, len(peers))
 
-    first = links.slots(3)
+    first = links.slots(5)
     away = device(dz=1)
     across = device(dz=1, dc=1)
-    links.start(swap_out.at[:, mine], swap_in.at[1], first + 1, away)
-    links.start(swap_out.at[:, other], swap_in.at[2], first + 2, across)
-    links.start(swap_out.at[:, other], swap_in.at[0], first, core)
-
-    def place(z, own, theirs):
-        own, theirs = own.astype(F32), theirs.astype(F32)
+    for n in (0, 1):
+        links.start(swap_out.at[n, c], swap_in.at[1, n], first + 1 + 2 * n, away)
+        links.start(swap_out.at[n, 1 - c], swap_in.at[2, n], first + 2 + 2 * n, across)
+        if n == 0:
+            links.start(swap_out.at[:, 1 - c], swap_in.at[0], first, core)
+
+    def place(buf, z, own, theirs):
+        own, theirs = unfold(own), unfold(theirs)
         low = jnp.where(c == 0, own, theirs)
         high = jnp.where(c == 0, theirs, own)
-        xb[y, z, x, :, mine] = jnp.concatenate([low[0:8], high[0:8]], axis=0).astype(BF)
-        gb[y, z, x, :, mine] = jnp.concatenate([low[8:16], high[8:16]], axis=0).astype(BF)
+        buf[y, z, x, :, mine] = jnp.concatenate([low, high], axis=0).astype(BF)
+
+    def place_far(n, buf):
+        links.arrived(swap_in.at[1, n], first + 1 + 2 * n, away)
+        links.arrived(swap_in.at[2, n], first + 2 + 2 * n, across)
+        place(buf, 1 - zh, swap_in[1, n], swap_in[2, n])
 
     links.arrived(swap_in.at[0], first, core)
-    place(zh, swap_out[:, mine], swap_in[0])
+    place(xb, zh, swap_out[0, c], swap_in[0, 0])
+    place(gb, zh, swap_out[1, c], swap_in[0, 1])
     def step_x(d):
         return device(dx=d)
 
@@ -210,10 +227,9 @@
     gg.send_first(0)
     gx.wait_first(0)
     gx.send_second(0)
-    links.arrived(swap_in.at[1], first + 1, away)
-    links.arrived(swap_in.at[2], first + 2, across)
-    place(1 - zh, swap_in[1], swap_in[2])
+    place_far(0, xb)
     gx.send_first(1)
+    place_far(1, gb)
     gg.send_first(1)
     gx.send_swap(0, 0)
     gg.wait_first(0)
@@ -316,10 +332,10 @@
     links.start(hb.at[yf], hb.at[yf], h3, partner)
 
     class Spread:
-        def __init__(self, part, core_in, ring_y, ring_x, then_x, then_y, got_x, got_y, zs, fr):
+        def __init__(self, part, core_in, ring_y, ring_x, then_x, then_y, got_x, got_y, zs, fr, fold_out, fold_in):
             self.part, self.core_in, self.ring_y, self.ring_x = part, core_in, ring_y, ring_x
             self.then_x, self.then_y, self.got_x, self.got_y = then_x, then_y, got_x, got_y
-            self.zs, self.fr = zs, fr
+            self.zs, self.fr, self.fold_out, self.fold_in = zs, fr, fold_out, fold_in
             self.cores, self.yx, self.xy = links.slots(4), links.slots(4), links.slots(16)
             self.x, self.y, self.z = links.slots(4), links.slots(4), links.slots(3)
 
@@ -376,16 +392,19 @@
             for d in (1, 2, 3):
                 total = total + self.got_y[d - 1].astype(F32)
             self.zs[:, :, right] = total
-            links.start(self.zs.at[1 - zh, rows_mine], self.fr.at[1], self.z + 1, away)
-            links.start(self.zs.at[1 - zh, rows_other], self.fr.at[2], self.z + 2, across)
-            links.start(self.zs.at[zh, rows_other], self.fr.at[0], self.z, core)
+            self.fold_out[0] = fold(self.zs[1 - zh, rows_mine, :])
+            self.fold_out[1] = fold(self.zs[1 - zh, rows_other, :])
+            links.start(self.fold_out.at[0], self.fold_in.at[0], self.z + 1, away)
+            links.start(self.fold_out.at[1], self.fold_in.at[1], self.z + 2, across)
+            links.start(self.zs.at[zh, rows_other], self.fr, self.z, core)
 
         def last(self, ref, scale):
-            links.arrived(self.fr.at[0], self.z, core)
-            links.arrived(self.fr.at[1], self.z + 1, away)
-            links.arrived(self.fr.at[2], self.z + 2, across)
-            ref[:, mine] = ((self.zs[zh, rows_mine, :] + self.fr[1]) * scale).astype(BF)
-            ref[:, other] = ((self.fr[0] + self.fr[2]) * scale).astype(BF)
+            links.arrived(self.fr, self.z, core)
+            links.arrived(self.fold_in.at[0], self.z + 1, away)
+            links.arrived(self.fold_in.at[1], self.z + 2, across)
+            own = self.zs[zh, rows_mine, :] + unfold(self.fold_in[0])
+            ref[:, mine] = (own * scale).astype(BF)
+            ref[:, other] = ((self.fr[...] + unfold(self.fold_in[1])) * scale).astype(BF)
 
         def finish(self):
             for d in (1, 2, 3):
@@ -424,7 +443,7 @@
     def down_tile(i, top):
         columns = pl.ds(pl.multiple_of(i * 256, 256), 256)
         rows = gb[:, :, :, :, columns].reshape(512, 256)
-        value = jnp.dot(hq_all, rows, preferred_element_type=F32) * (s1 * s2)
+        value = jnp.dot(hq_all, rows, preferred_element_type=F32)
         down_g[:, columns] = value.astype(BF)
         return jnp.maximum(top, jnp.max(jnp.abs(value)))
 
@@ -446,7 +465,7 @@
     def wide_tile(i, top):
         columns = pl.ds(pl.multiple_of(i * 256, 256), 256)
         rows = xb[:, :, :, :, columns].reshape(512, 256)
-        value = jnp.dot(dq_all, rows, preferred_element_type=F32) * (s0 * s3)
+        value = jnp.dot(dq_all, rows, preferred_element_type=F32)
         wide_g[:, columns] = value.astype(BF)
         return jnp.maximum(top, jnp.max(jnp.abs(value)))
 
@@ -457,8 +476,10 @@
     store_w.start()
 
     row = lax.broadcasted_iota(jnp.int32, (8, 128), 0)
+    by_wide, by_down = s0 * s3, s1 * s2
+    marks = (max_x, max_h, max_g, max_p, max_w * by_wide, max_d * by_down, by_wide, by_down)
     tops = jnp.zeros((8, 128), F32)
-    for n, value in enumerate((max_x, max_h, max_g, max_p, max_w, max_d)):
+    for n, value in enumerate(marks):
         tops = jnp.where(row == n, value, tops)
 
     def send_tops(stage, value, offsets):
@@ -502,9 +523,9 @@
 
 
 def scale_grads(
-    peaks, out_in, in_grad_in, wide_hbm, wdown_hbm,
+    peaks_hbm, out_in, in_grad_in, wide_hbm, wdown_hbm,
     gate_out, up_out, down_out, out_ref, in_grad_ref, amaxes_ref,
-    held, scaled, load_sem, store_sem,
+    held, scaled, peaks, load_sem, store_sem,
 ):
     sources = [wide_hbm.at[pl.ds(0, UNITS)], wide_hbm.at[pl.ds(UNITS, UNITS)], wdown_hbm]
     targets = [gate_out, up_out, down_out]
@@ -515,20 +536,27 @@
         pltpu.make_async_copy(scaled.at[n], target, store_sem.at[n])
         for n, target in enumerate(targets)
     ]
+    peaks_load = pltpu.make_async_copy(peaks_hbm, peaks, load_sem.at[3])
+    peaks_load.start()
     for load in loads:
         load.start()
+    passed = [
+        pltpu.make_async_copy(out_in, out_ref, store_sem.at[3]),
+        pltpu.make_async_copy(in_grad_in, in_grad_ref, store_sem.at[4]),
+    ]
+    for copy in passed:
+        copy.start()
+    peaks_load.wait()
     for n in range(6):
         amaxes_ref[n] = peaks[8 + n, 0]
-    out_ref[...] = out_in[...]
-    in_grad_ref[...] = in_grad_in[...]
-    over_wide = 1.0 / (peaks[4, 0] + 1e-6)
-    over_down = 1.0 / (peaks[5, 0] + 1e-6)
+    over_wide = peaks[6, 0] / (peaks[4, 0] + 1e-6)
+    over_down = peaks[7, 0] / (peaks[5, 0] + 1e-6)
     for n in range(3):
         loads[n].wait()
         over = over_wide if n < 2 else over_down
         scaled[n] = (held[n].astype(F32) * over).astype(BF)
         stores[n].start()
-    for store in stores:
+    for store in stores + passed:
         store.wait()
 
 
@@ -541,7 +569,7 @@
         V((3, 2, 4, 16, 512), BF), V((3, 4, 2, 16, 512), BF),
         V((2, 4, 16, 512), BF), V((4, 2, 16, 512), BF),
         V((3, 2, 16, 512), BF), V((3, 2, 16, 512), BF),
-        V((2, 16, HALF), F32), V((3, 8, HALF), F32),
+        V((2, 16, HALF), F32), V((8, HALF), F32), V((2, 16, 512), BF), V((2, 16, 512), BF),
     )
     output, input_grad, wide, wdown, peaks = pl.pallas_call(
         kernel,
@@ -557,7 +585,7 @@
         scratch_shapes=[
             V((4, 2, 4, 16, 2048), BF), V((4, 2, 4, 16, 2048), BF),
             V((WIDE, 2048), BF), V((UNITS, 2048), BF),
-            V((16, 2048), BF), V((3, 16, HALF), BF),
+            V((2, 2, 16, 512), BF), V((3, 2, 16, 512), BF),
             V((2, 2, UNITS, 128), BF), V((2, 2, UNITS, 128), F32), V((2, 2, UNITS, 128), BF),
             V((2, UNITS, 128), BF), V((2, UNITS, 128), BF),
             V((2, UNITS, 128), BF), V((2, UNITS, 128), F32), V((2, UNITS, 128), BF),
@@ -586,13 +614,14 @@
     gate_grad, up_grad, down_grad, output, input_grad, amaxes = pl.pallas_call(
         scale_grads,
         out_shape=full,
-        in_specs=[smem, vmem, vmem, hbm, hbm],
-        out_specs=(hbm, hbm, hbm, vmem, vmem, smem),
+        in_specs=[hbm] * 5,
+        out_specs=(hbm, hbm, hbm, hbm, hbm, smem),
         scratch_shapes=[
             V((3, UNITS, 2048), BF),
             V((3, UNITS, 2048), BF),
-            pltpu.SemaphoreType.DMA((3,)),
-            pltpu.SemaphoreType.DMA((3,)),
+            pltpu.SMEM((16, 128), F32),
+            pltpu.SemaphoreType.DMA((4,)),
+            pltpu.SemaphoreType.DMA((5,)),
         ],
         compiler_params=pltpu.CompilerParams(vmem_limit_bytes=60 << 20),
         name="scale",

time: 103 us -> 101 us (0.981)
  no operation moved by 1% of the time
where the time goes in v5:
time: 101 us
  Pallas kernels  100 us (99%)
    pallas_call x1, Pallas kernels, shards(): pl.pallas_call(kernel, out_shape=(jax.ShapeDtypeStruct((8, 2048), BF), ja...  95.4 us
    pallas_call x1, Pallas kernels, shards(): pl.pallas_call(scale_grads, out_shape=full, in_specs=[hbm] * 5, out_specs...  4.64 us

profile of v5, /device:TPU:1, one launch (start us, length us, event | category | flops | bytes accessed | tf_op | source)
XLA Modules:
  0.0 100.8 jit_solution(434415417269517521)
XLA Ops:
  0.6 95.4 %layer.1 = (bf16[8,2048]{1,0:T(8,128)(2,1)}, bf16[8,2048]{1,0:T(8,128)(2,1)}, bf16[832,2048]{1,0:T(8,128)(2,1)}, bf16[416,2048]{1,0:T(8,128)(2,1)}, f32[16,128]{1,0:T(8,128)}) custom-call(f32[4]{0:T(128)} %prior.1, bf16[8,2048]{1,0:T(8,128)(2,1)} %tokens.1, bf16[8,2048]{1,0:T(8,128)(2,1)} %out_grad.1, bf16[416,2048]{1,0:T(8,128)(2,1)} %bitcast.4, ...), custom_call_target="tpu_custom_call" | custom-call | tf_op jit(solution)/shard_map/layer/pallas_call | solution.py:574
  96.0 4.6 %scale.1 = (bf16[416,2048]{1,0:T(8,128)(2,1)}, bf16[416,2048]{1,0:T(8,128)(2,1)}, bf16[416,2048]{1,0:T(8,128)(2,1)}, bf16[8,2048]{1,0:T(8,128)(2,1)}, bf16[8,2048]{1,0:T(8,128)(2,1)}, /*index=5*/f32[6]{0:T(128)}) custom-call(f32[16,128]{1,0:T(8,128)} %get-tuple-element.17.peaks_hbm, bf16[8,2048]{1,0:T(8,128)(2,1)} %get-tuple-element.18.out_in, ...), custom_call_target="tpu_custom_call" | custom-call | tf_op jit(solution)/shard_map/scale/pallas_call | solution.py:614

commit v6 on v5

--- a/solution.py
+++ b/solution.py
@@ -441,18 +441,18 @@
     hq_all = jnp.concatenate([hb[n] for n in range(4)], axis=1)
 
     def down_tile(i, top):
-        columns = pl.ds(pl.multiple_of(i * 256, 256), 256)
-        rows = gb[:, :, :, :, columns].reshape(512, 256)
+        columns = pl.ds(pl.multiple_of(i * 512, 512), 512)
+        rows = gb[:, :, :, :, columns].reshape(512, 512)
         value = jnp.dot(hq_all, rows, preferred_element_type=F32)
         down_g[:, columns] = value.astype(BF)
         return jnp.maximum(top, jnp.max(jnp.abs(value)))
 
-    max_d = lax.fori_loop(0, 4, down_tile, jnp.float32(0.0))
+    max_d = lax.fori_loop(0, 2, down_tile, jnp.float32(0.0))
     out_sum.first(3)
     for u in (0, 1):
         links.arrived(db.at[yp, units[u]], g2 + u, partner)
     in_sum.block(2, db[yp], wide_w[...])
-    max_d = lax.fori_loop(4, 8, down_tile, max_d)
+    max_d = lax.fori_loop(2, 4, down_tile, max_d)
     store_d = pltpu.make_async_copy(down_g, wdown_hbm, store_sem.at[0])
     store_d.start()
     in_sum.first(2)
@@ -463,15 +463,15 @@
     dq_all = jnp.concatenate([db[n] for n in range(4)], axis=1)
 
     def wide_tile(i, top):
-        columns = pl.ds(pl.multiple_of(i * 256, 256), 256)
-        rows = xb[:, :, :, :, columns].reshape(512, 256)
+        columns = pl.ds(pl.multiple_of(i * 512, 512), 512)
+        rows = xb[:, :, :, :, columns].reshape(512, 512)
         value = jnp.dot(dq_all, rows, preferred_element_type=F32)
         wide_g[:, columns] = value.astype(BF)
         return jnp.maximum(top, jnp.max(jnp.abs(value)))
 
-    max_w = lax.fori_loop(0, 4, wide_tile, jnp.float32(0.0))
+    max_w = lax.fori_loop(0, 2, wide_tile, jnp.float32(0.0))
     in_sum.first(3)
-    max_w = lax.fori_loop(4, 8, wide_tile, max_w)
+    max_w = lax.fori_loop(2, 4, wide_tile, max_w)
     store_w = pltpu.make_async_copy(wide_g, wide_hbm, store_sem.at[1])
     store_w.start()
 

time: 101 us -> 99.8 us (0.988)
  Pallas kernels: 100 us -> 98.9 us
    pallas_call x1, Pallas kernels: 95.4 us -> 94.3 us  [shards(): pl.pallas_call(kernel, out_shape=(jax.ShapeDtypeStruct((8, 2048), BF), ja...]
where the time goes in v6:
time: 99.8 us; the launch traced here: 99.7 us
  Pallas kernels  98.9 us (99%)
    pallas_call x1, Pallas kernels, shards(): pl.pallas_call(kernel, out_shape=(jax.ShapeDtypeStruct((8, 2048), BF), ja...  94.3 us
    pallas_call x1, Pallas kernels, shards(): pl.pallas_call(scale_grads, out_shape=full, in_specs=[hbm] * 5, out_specs...  4.64 us

profile of v6, /device:TPU:1, one launch (start us, length us, event | category | flops | bytes accessed | tf_op | source)
XLA Modules:
  0.0 99.7 jit_solution(13154674203287913623)
XLA Ops:
  0.6 94.3 %layer.1 = (bf16[8,2048]{1,0:T(8,128)(2,1)}, bf16[8,2048]{1,0:T(8,128)(2,1)}, bf16[832,2048]{1,0:T(8,128)(2,1)}, bf16[416,2048]{1,0:T(8,128)(2,1)}, f32[16,128]{1,0:T(8,128)}) custom-call(f32[4]{0:T(128)} %prior.1, bf16[8,2048]{1,0:T(8,128)(2,1)} %tokens.1, bf16[8,2048]{1,0:T(8,128)(2,1)} %out_grad.1, bf16[416,2048]{1,0:T(8,128)(2,1)} %bitcast.4, ...), custom_call_target="tpu_custom_call" | custom-call | tf_op jit(solution)/shard_map/layer/pallas_call | solution.py:574
  94.9 4.6 %scale.1 = (bf16[416,2048]{1,0:T(8,128)(2,1)}, bf16[416,2048]{1,0:T(8,128)(2,1)}, bf16[416,2048]{1,0:T(8,128)(2,1)}, bf16[8,2048]{1,0:T(8,128)(2,1)}, bf16[8,2048]{1,0:T(8,128)(2,1)}, /*index=5*/f32[6]{0:T(128)}) custom-call(f32[16,128]{1,0:T(8,128)} %get-tuple-element.17.peaks_hbm, bf16[8,2048]{1,0:T(8,128)(2,1)} %get-tuple-element.18.out_in, ...), custom_call_target="tpu_custom_call" | custom-call | tf_op jit(solution)/shard_map/scale/pallas_call | solution.py:614
